TPU v7x, 128 devices: a whole 4x4x4 slice. The times are simulated.
128 devices in a mesh: section: 2 (over core), expert: 16 (over y, z), dp: 4 (over x).
Axes of the slice: x: 4, y: 4, z: 4, core: 2. Of those that a mesh axis runs over, the one named last changes fastest.
Arguments:
- inputs: bfloat16 [2, 9600, 512], P(None, ('expert', 'dp')), may hold values from -16 to 16
- cotangent: bfloat16 [2, 9600, 512], P(None, ('expert', 'dp')), may hold values from -6 to 6
- norm_gains: float32 [2, 2, 512], P('section'), may hold values from 0.25 to 1.75
- norm_biases: float32 [2, 2, 512], P('section'), may hold values from -1.2 to 1.2
- w_qkv: bfloat16 [2, 512, 1536], P('section'), may hold values from -0.375 to 0.375
- w_attn_out: bfloat16 [2, 512, 512], P('section'), may hold values from -0.75 to 0.75
- w_router: bfloat16 [2, 512, 16], P('section'), may hold values from -0.1875 to 0.1875
- w_expert_in: bfloat16 [2, 16, 512, 2048], P('section', 'expert', None, 'dp'), may hold values from -0.25 to 0.25
- w_expert_out: bfloat16 [2, 16, 2048, 512], P('section', 'expert', 'dp'), may hold values from -0.25 to 0.25
- routes: int32 [2, 2, 9600, 2], P('section', None, ('expert', 'dp')), may hold values from 0 to 15, all different within a row; in each aligned block of 150 rows (0 to 149, 150 to 299, ..., all dimensions but the last counted through in order) at most 24 rows name the same one
Outputs:
- layer_outputs: bfloat16 [2, 2, 9600, 512], P('section', None, ('expert', 'dp'))
- layer_input_grads: bfloat16 [2, 2, 9600, 512], P('section', None, ('expert', 'dp'))
- grad_norm_gains: float32 [2, 2, 512], P('section', None, ('expert', 'dp'))
- grad_norm_biases: float32 [2, 2, 512], P('section', None, ('expert', 'dp'))
- grad_qkv: float32 [2, 512, 1536], P('section', ('expert', 'dp'))
- grad_attn_out: float32 [2, 512, 512], P('section', ('expert', 'dp'))
- grad_router: float32 [2, 512, 16], P('section', ('expert', 'dp'))
- grad_expert_in: float32 [2, 16, 512, 2048], P('section', 'expert', None, 'dp')
- grad_expert_out: float32 [2, 16, 2048, 512], P('section', 'expert', 'dp')
Inputs may be any that keep to these rules, and one draw needn't show every extreme that they name: `routes`: in each aligned block of 150 rows (one device's tokens of one layer and micro-batch) the two entries of a row differ and no expert is named by more than 24 entries.
All inputs are finite; a program needn't handle non-finite values.
Results may differ from a plain program's by a relative error of at most 0.033.
Values may be sent and summed in bfloat16 or wider, within the bound.
A program may use at most 192 MiB of HBM per device.

v0:
```python
from functools import partial

import jax
import jax.numpy as jnp
from jax import lax
from jax.sharding import PartitionSpec as P

HEADS = 8
HEAD_DIM = 64
SEQ = 50


EPSILON = 1e-06
HIGHEST = lax.Precision.HIGHEST


def shifted(shard, axis, by):
    size = lax.axis_size(axis)
    pairs = [(i, i + by) for i in range(size) if 0 <= i + by < size]
    return lax.ppermute(shard, axis, pairs)


def norm_apply(values, norm_gain, offset):
    center = values - jnp.mean(values, -1, keepdims=True)
    spread = jnp.mean(center * center, -1, keepdims=True)
    return center * lax.rsqrt(spread + EPSILON) * norm_gain + offset


def slot_rows(chosen, experts):
    blocks = chosen.shape[0]
    flattened = chosen.reshape(blocks, -1)
    matches = (flattened[:, :, None] == jnp.arange(experts, dtype=jnp.int32)).astype(jnp.int32)
    running = jnp.cumsum(matches, axis=1, dtype=jnp.int32)
    position = jnp.sum(running * matches, axis=2, dtype=jnp.int32) - 1
    return position.reshape(chosen.shape)


def gate_values(logits, chosen):
    picked = jnp.take_along_axis(jax.nn.softmax(logits, axis=-1), chosen, axis=1)
    return picked / jnp.sum(picked, axis=1, keepdims=True)


def split_heads(packed, images):
    features = packed.shape[1] // 3
    return [
        packed[:, member * features : (member + 1) * features].reshape(images, SEQ, HEADS, HEAD_DIM)
        for member in range(3)
    ]


def owner_rows(arrived, per_owner):
    sources = arrived.shape[0]
    features = arrived.shape[2]
    return (
        arrived.reshape(sources, per_owner, -1, features)
        .transpose(1, 0, 2, 3)
        .reshape(per_owner, -1, features)
    )


def source_rows(finished, sources):
    per_owner = finished.shape[0]
    features = finished.shape[2]
    return (
        finished.reshape(per_owner, sources, -1, features)
        .transpose(1, 0, 2, 3)
        .reshape(sources, -1, features)
    )


def attend_forward(states, norm_gain, offset, qkv_weight, out_weight):
    tokens, features = states.shape
    images = tokens // SEQ
    normed = norm_apply(states, norm_gain, offset).astype(jnp.bfloat16)
    packed = jnp.dot(normed, qkv_weight, preferred_element_type=jnp.float32).astype(jnp.bfloat16)
    queries, key_rows, value_rows = split_heads(packed, images)
    scores = jnp.einsum(
        "bqhd,bkhd->bhqk", queries, key_rows, preferred_element_type=jnp.float32
    ) * HEAD_DIM ** (-0.5)
    highest_score = jnp.max(scores, axis=-1, keepdims=True)
    log_total = highest_score + jnp.log(
        jnp.sum(jnp.exp(scores - highest_score), axis=-1, keepdims=True)
    )
    shares = jnp.exp(scores - log_total).astype(jnp.bfloat16)
    blended = jnp.einsum("bhqk,bkhd->bqhd", shares, value_rows, preferred_element_type=jnp.float32)
    blended = blended.reshape(tokens, features).astype(jnp.bfloat16)
    attended = states + jnp.dot(blended, out_weight, preferred_element_type=jnp.float32)
    return (attended, (normed, packed, log_total, blended))


def attend_backward(grad_attended, kept, states, norm_gain, offset, qkv_weight, out_weight):
    normed, packed, log_total, blended = kept
    tokens, features = states.shape
    images = tokens // SEQ
    scale = HEAD_DIM ** (-0.5)
    grad_branch = grad_attended.astype(jnp.bfloat16)
    grad_out_weight = jnp.dot(blended.T, grad_branch, preferred_element_type=jnp.float32)
    grad_blended = jnp.dot(grad_branch, out_weight.T, preferred_element_type=jnp.float32).astype(
        jnp.bfloat16
    )
    grad_blended = grad_blended.reshape(images, SEQ, HEADS, HEAD_DIM)
    queries, key_rows, value_rows = split_heads(packed, images)
    scores = (
        jnp.einsum("bqhd,bkhd->bhqk", queries, key_rows, preferred_element_type=jnp.float32) * scale
    )
    shares = jnp.exp(scores - log_total)
    grad_shares = jnp.einsum(
        "bqhd,bkhd->bhqk", grad_blended, value_rows, preferred_element_type=jnp.float32
    )
    grad_value = jnp.einsum(
        "bhqk,bqhd->bkhd",
        shares.astype(jnp.bfloat16),
        grad_blended,
        preferred_element_type=jnp.float32,
    )
    grad_scores = shares * (grad_shares - jnp.sum(shares * grad_shares, axis=-1, keepdims=True))
    grad_scores = grad_scores.astype(jnp.bfloat16)
    grad_query = (
        jnp.einsum("bhqk,bkhd->bqhd", grad_scores, key_rows, preferred_element_type=jnp.float32)
        * scale
    )
    grad_key = (
        jnp.einsum("bhqk,bqhd->bkhd", grad_scores, queries, preferred_element_type=jnp.float32)
        * scale
    )
    grad_packed = jnp.concatenate(
        [member.reshape(tokens, features) for member in (grad_query, grad_key, grad_value)], axis=1
    )
    grad_packed = grad_packed.astype(jnp.bfloat16)
    grad_qkv_weight = jnp.dot(normed.T, grad_packed, preferred_element_type=jnp.float32)
    grad_normed = jnp.dot(grad_packed, qkv_weight.T, preferred_element_type=jnp.float32)
    _, norm_back = jax.vjp(norm_apply, states, norm_gain, offset)
    grad_states, grad_gain, grad_offset = norm_back(grad_normed)
    return (grad_attended + grad_states, grad_gain, grad_offset, grad_qkv_weight, grad_out_weight)


def local(
    inputs,
    cotangent,
    norm_gains,
    norm_biases,
    w_qkv,
    w_attn_out,
    w_router,
    w_expert_in,
    w_expert_out,
    routes,
):
    gain_pair = norm_gains[0]
    offset_pair = norm_biases[0]
    qkv_weight = w_qkv[0]
    out_weight = w_attn_out[0]
    router_weight = w_router[0]
    expert_in = w_expert_in[0]
    expert_out = w_expert_out[0]
    route_table = routes[0]
    micro = inputs.shape[0]
    tokens = inputs.shape[1]
    features = inputs.shape[2]
    experts = router_weight.shape[1]
    per_owner = expert_in.shape[0]
    owners = experts // per_owner
    capacity = 5 * tokens // (2 * experts) + 1
    section_number = lax.axis_index("section")
    first = section_number == 0
    use_in, use_out = (expert_in, expert_out)

    def experts_backward(send, kept_rows):
        every, before, hidden = kept_rows
        arrived = lax.all_to_all(
            send.reshape(owners, -1, features), "expert", split_axis=0, concat_axis=0, tiled=True
        )
        grad_finished = owner_rows(arrived, per_owner)
        grad_every = lax.all_gather(grad_finished, "dp", axis=1, tiled=True)
        grad_hidden = jnp.einsum(
            "erd,efd->erf", grad_every, use_out, preferred_element_type=jnp.float32
        )
        _, gelu_back = jax.vjp(partial(jax.nn.gelu, approximate=False), before)
        grad_before = gelu_back(grad_hidden)[0].astype(jnp.bfloat16)
        grad_win = jnp.einsum(
            "erd,erf->edf", every, grad_before, preferred_element_type=jnp.float32
        )
        grad_wout = jnp.einsum(
            "erf,erd->efd", hidden, grad_every, preferred_element_type=jnp.float32
        )
        grad_rows = jnp.einsum(
            "erf,edf->erd", grad_before, use_in, preferred_element_type=jnp.float32
        )
        grad_sent = lax.psum_scatter(grad_rows, "dp", scatter_dimension=1, tiled=True).astype(
            jnp.bfloat16
        )
        back_rows = lax.all_to_all(
            source_rows(grad_sent, owners), "expert", split_axis=0, concat_axis=0, tiled=True
        )
        return (back_rows.reshape(-1, features), grad_win, grad_wout)

    def layer_backward(grad_result, kept):
        current, attended, attn_kept, normed, logits, gates, chosen, target, picked, expert_kept = (
            kept
        )
        grad_gates = jnp.sum(grad_result[:, None, :] * picked.astype(jnp.float32), axis=2)
        grad_slots = (gates[:, :, None] * grad_result[:, None, :]).astype(jnp.bfloat16)
        send = jnp.zeros((experts * capacity, features), jnp.bfloat16)
        send = send.at[target.reshape(-1)].set(grad_slots.reshape(-1, features))
        back_rows, grad_win, grad_wout = experts_backward(send, expert_kept)
        grad_copies = jnp.sum(back_rows[target].astype(jnp.float32), axis=1)
        _, gate_back = jax.vjp(partial(gate_values, chosen=chosen), logits)
        grad_logits = gate_back(grad_gates)[0]
        grad_route_weight = jnp.dot(normed.astype(jnp.float32).T, grad_logits, precision=HIGHEST)
        grad_normed = grad_copies + jnp.dot(
            grad_logits, router_weight.astype(jnp.float32).T, precision=HIGHEST
        )
        _, norm_back = jax.vjp(norm_apply, attended, gain_pair[1], offset_pair[1])
        grad_inner, gain_late, offset_late = norm_back(grad_normed)
        grad_attended = grad_result + grad_inner
        grad_states, gain_early, offset_early, grad_qkv_weight, grad_out_weight = attend_backward(
            grad_attended,
            attn_kept,
            current.astype(jnp.float32),
            gain_pair[0],
            offset_pair[0],
            qkv_weight,
            out_weight,
        )
        dense_terms = (
            grad_qkv_weight,
            grad_out_weight,
            grad_route_weight,
            jnp.stack([gain_early, gain_late]),
            jnp.stack([offset_early, offset_late]),
        )
        return (grad_states, dense_terms, grad_win, grad_wout)

    arriving = jnp.zeros((tokens, features), jnp.bfloat16)
    produced = []
    saved_steps = []
    for moment in range(micro + 1):
        order = jnp.clip(moment - section_number, 0, micro - 1)
        current = jnp.where(first, inputs[min(moment, micro - 1)], arriving)
        chosen = lax.dynamic_index_in_dim(route_table, order, 0, keepdims=False)
        states = current.astype(jnp.float32)
        layer_attended, layer_attn_kept = attend_forward(
            states, gain_pair[0], offset_pair[0], qkv_weight, out_weight
        )
        layer_normed = norm_apply(layer_attended, gain_pair[1], offset_pair[1]).astype(jnp.bfloat16)
        layer_logits = jnp.dot(layer_normed, router_weight, preferred_element_type=jnp.float32)
        layer_gates = gate_values(layer_logits, chosen)
        layer_target = chosen * capacity + slot_rows(chosen[None], experts)[0]
        layer_send = jnp.zeros((experts * capacity, features), jnp.bfloat16)
        layer_send = layer_send.at[layer_target.reshape(-1)].set(
            jnp.repeat(layer_normed, 2, axis=0)
        )
        experts_arrived = lax.all_to_all(
            layer_send.reshape(owners, -1, features),
            "expert",
            split_axis=0,
            concat_axis=0,
            tiled=True,
        )
        own_rows = owner_rows(experts_arrived, per_owner)
        experts_every = lax.all_gather(own_rows, "dp", axis=1, tiled=True)
        experts_before = jnp.einsum(
            "erd,edf->erf", experts_every, use_in, preferred_element_type=jnp.float32
        )
        experts_hidden = jax.nn.gelu(experts_before, approximate=False).astype(jnp.bfloat16)
        term_out = jnp.einsum(
            "erf,efd->erd", experts_hidden, use_out, preferred_element_type=jnp.float32
        )
        finished = lax.psum_scatter(term_out, "dp", scatter_dimension=1, tiled=True).astype(
            jnp.bfloat16
        )
        experts_back_rows = lax.all_to_all(
            source_rows(finished, owners), "expert", split_axis=0, concat_axis=0, tiled=True
        )
        layer_back_rows = experts_back_rows.reshape(-1, features)
        layer_expert_kept = (experts_every, experts_before, experts_hidden)
        layer_picked = layer_back_rows[layer_target]
        result = layer_attended + jnp.sum(
            layer_gates[:, :, None] * layer_picked.astype(jnp.float32), axis=1
        )
        layer_kept = (
            current,
            layer_attended,
            layer_attn_kept,
            layer_normed,
            layer_logits,
            layer_gates,
            chosen,
            layer_target,
            layer_picked,
            layer_expert_kept,
        )
        result, kept = (result.astype(jnp.bfloat16), layer_kept)
        produced.append(result)
        saved_steps.append(kept)
        if moment < micro:
            arriving = shifted(result, "section", 1)
    dense_total = None
    win_total = None
    wout_total = None
    sent_grads = []
    grad_arriving = jnp.zeros((tokens, features), jnp.bfloat16)
    for moment in range(micro + 1):
        early = saved_steps[max(moment - 1, 0)]
        late = saved_steps[min(moment + 1, micro)]
        kept = jax.tree.map(lambda one, two: jnp.where(first, one, two), early, late)
        live = jnp.where(first, moment >= 1, moment < micro)
        incoming = jnp.where(first, grad_arriving, cotangent[min(moment, micro - 1)]).astype(
            jnp.float32
        )
        grad_result = jnp.where(live, incoming, 0.0)
        grad_states, dense_terms, grad_win, grad_wout = layer_backward(grad_result, kept)
        if dense_total is None:
            dense_total, win_total, wout_total = (dense_terms, grad_win, grad_wout)
        else:
            dense_total = tuple((total + term for total, term in zip(dense_total, dense_terms)))
            win_total = win_total + grad_win
            wout_total = wout_total + grad_wout
        grad_sent = grad_states.astype(jnp.bfloat16)
        sent_grads.append(grad_sent)
        if moment < micro:
            grad_arriving = shifted(grad_sent, "section", -1)
    qkv_total, attn_total, route_total, gain_total, offset_total = dense_total
    qkv_sum, attn_sum, route_sum, gain_sum, offset_sum = (
        lax.psum_scatter(qkv_total, ("expert", "dp"), scatter_dimension=0, tiled=True),
        lax.psum_scatter(attn_total, ("expert", "dp"), scatter_dimension=0, tiled=True),
        lax.psum_scatter(route_total, ("expert", "dp"), scatter_dimension=0, tiled=True),
        lax.psum_scatter(gain_total, ("expert", "dp"), scatter_dimension=1, tiled=True),
        lax.psum_scatter(offset_total, ("expert", "dp"), scatter_dimension=1, tiled=True),
    )
    win_share, wout_share = (win_total, wout_total)
    layer_outputs = jnp.stack(
        [jnp.where(first, produced[number], produced[number + 1]) for number in range(micro)]
    )
    layer_input_grads = jnp.stack(
        [jnp.where(first, sent_grads[number + 1], sent_grads[number]) for number in range(micro)]
    )
    return (
        layer_outputs[None],
        layer_input_grads[None],
        gain_sum[None],
        offset_sum[None],
        qkv_sum[None],
        attn_sum[None],
        route_sum[None],
        win_share[None],
        wout_share[None],
    )


def solution(mesh):
    return jax.shard_map(
        local,
        mesh=mesh,
        in_specs=(
            P(None, ("expert", "dp"), None),
            P(None, ("expert", "dp"), None),
            P("section", None, None),
            P("section", None, None),
            P("section", None, None),
            P("section", None, None),
            P("section", None, None),
            P("section", "expert", None, "dp"),
            P("section", "expert", "dp", None),
            P("section", None, ("expert", "dp"), None),
        ),
        out_specs=(
            P("section", None, ("expert", "dp"), None),
            P("section", None, ("expert", "dp"), None),
            P("section", None, ("expert", "dp")),
            P("section", None, ("expert", "dp")),
            P("section", ("expert", "dp"), None),
            P("section", ("expert", "dp"), None),
            P("section", ("expert", "dp"), None),
            P("section", "expert", None, "dp"),
            P("section", "expert", "dp", None),
        ),
        check_vma=False,
    )
```

profile of v0, /device:TPU:0, one launch (start us, length us, event | category | flops | bytes accessed | tf_op | source)
XLA Modules:
  0.0 1396.6 jit_solution(17861822114086249457)
XLA Ops:
  37.4 18.1 %all_to_all.60 = bf16[16,24,512]{2,1,0:T(8,128)(2,1)} all-to-all(bf16[16,24,512]{2,1,0:T(8,128)(2,1)} %bitcast.574), channel_id=1, replica_groups=mesh['section'=2,'expert'=16,'dp'=4] {'expert'}, dimensions={0} | all-to-all | bytes 786432 | tf_op jit(solution)/shard_map/all_to_all | solution.py:253
  55.7 24.5 %all-gather.7.cloned.1.call-done = bf16[1,1536,512]{2,1,0:T(8,128)(2,1)} async-done(((bf16[1,384,512]{2,1,0:T(8,128)(2,1)}), bf16[1,1536,512]{2,1,0:T(8,128)(2,1)}) %all-gather.7.cloned.1.call-update) | async-done | bytes 1572880 | tf_op jit(solution)/shard_map/all_gather | solution.py:261
  80.2 9.7 fusion.2
  96.6 36.6 %reduce-scatter.11.cloned.1.call-done = f32[1,384,512]{2,1,0:T(8,128)} async-done(((f32[1,1536,512]{2,1,0:T(8,128)}), f32[1,384,512]{2,1,0:T(8,128)}) %reduce-scatter.11.cloned.1.call-update) | async-done | bytes 786448 | tf_op jit(solution)/shard_map/reduce_scatter | solution.py:269
  180.1 14.8 %all_to_all.61 = bf16[16,24,512]{2,1,0:T(8,128)(2,1)} all-to-all(bf16[16,24,512]{2,1,0:T(8,128)(2,1)} %bitcast.575), channel_id=1, replica_groups=mesh['section'=2,'expert'=16,'dp'=4] {'expert'}, dimensions={0} | all-to-all | bytes 786432 | tf_op jit(solution)/shard_map/all_to_all | solution.py:253
  195.0 23.1 %all-gather.9.cloned.1.call-done = bf16[1,1536,512]{2,1,0:T(8,128)(2,1)} async-done(((bf16[1,384,512]{2,1,0:T(8,128)(2,1)}), bf16[1,1536,512]{2,1,0:T(8,128)(2,1)}) %all-gather.9.cloned.1.call-update) | async-done | bytes 1572880 | tf_op jit(solution)/shard_map/all_gather | solution.py:261
  218.1 9.8 fusion.5
  241.1 29.1 %reduce-scatter.13.cloned.1.call-done = f32[1,384,512]{2,1,0:T(8,128)} async-done(((f32[1,1536,512]{2,1,0:T(8,128)}), f32[1,384,512]{2,1,0:T(8,128)}) %reduce-scatter.13.cloned.1.call-update) | async-done | bytes 786448 | tf_op jit(solution)/shard_map/reduce_scatter | solution.py:269
  332.6 17.4 %all_to_all.62 = bf16[16,24,512]{2,1,0:T(8,128)(2,1)} all-to-all(bf16[16,24,512]{2,1,0:T(8,128)(2,1)S(1)} %bitcast.576), channel_id=1, replica_groups=mesh['section'=2,'expert'=16,'dp'=4] {'expert'}, dimensions={0} | all-to-all | bytes 786432 | tf_op jit(solution)/shard_map/all_to_all | solution.py:253
  350.3 9.9 fusion.13
  373.2 9.8 fusion.8
  388.5 25.5 %reduce-scatter.17.cloned.1.call-done = f32[1,384,512]{2,1,0:T(8,128)} async-done(((f32[1,1536,512]{2,1,0:T(8,128)}), f32[1,384,512]{2,1,0:T(8,128)}) %reduce-scatter.17.cloned.1.call-update) | async-done | bytes 786448 | tf_op jit(solution)/shard_map/reduce_scatter | solution.py:189
  482.3 16.8 %scatter_fusion = f32[150,16]{0,1:T(8,128)S(1)} fusion(f32[150,16]{0,1:T(8,128)S(1)} %broadcast_in_dim.85.clone, s32[300]{0:T(512)S(1)} %reshape.2212, f32[300]{0:T(512)S(1)} %reshape.2214), kind=kCustom, calls=%fused_computation.18 | custom fusion | flops 300 | bytes 6000 | tf_op jit(solution)/shard_map/transpose(jvp(jit(take_along_axis)))/scatter-add | solution.py:39
  531.1 16.1 %all_to_all.63 = bf16[16,24,512]{2,1,0:T(8,128)(2,1)} all-to-all(bf16[16,24,512]{2,1,0:T(8,128)(2,1)S(1)} %bitcast.573), channel_id=1, replica_groups=mesh['section'=2,'expert'=16,'dp'=4] {'expert'}, dimensions={0} | all-to-all | bytes 786432 | tf_op jit(solution)/shard_map/all_to_all | solution.py:170
  547.7 22.7 %all-gather.15.cloned.1.call-done = bf16[1,1536,512]{2,1,0:T(8,128)(2,1)} async-done(((bf16[1,384,512]{2,1,0:T(8,128)(2,1)}), bf16[1,1536,512]{2,1,0:T(8,128)(2,1)}) %all-gather.15.cloned.1.call-update) | async-done | bytes 1572880 | tf_op jit(solution)/shard_map/all_gather | solution.py:174
  570.4 9.9 fusion.18
  602.2 20.5 %reduce-scatter.19.cloned.1.call-done = f32[1,384,512]{2,1,0:T(8,128)} async-done(((f32[1,1536,512]{2,1,0:T(8,128)}), f32[1,384,512]{2,1,0:T(8,128)}) %reduce-scatter.19.cloned.1.call-update) | async-done | bytes 786448 | tf_op jit(solution)/shard_map/reduce_scatter | solution.py:189
  634.1 16.8 %scatter_fusion.1 = f32[150,16]{0,1:T(8,128)S(1)} fusion(f32[150,16]{0,1:T(8,128)S(1)} %broadcast_in_dim.85.clone.1, s32[300]{0:T(512)S(1)} %reshape.2218, f32[300]{0:T(512)S(1)} %reshape.2220), kind=kCustom, calls=%fused_computation.19 | custom fusion | flops 300 | bytes 6000 | tf_op jit(solution)/shard_map/transpose(jvp(jit(take_along_axis)))/scatter-add | solution.py:39
  683.6 17.3 %all_to_all.64 = bf16[16,24,512]{2,1,0:T(8,128)(2,1)} all-to-all(bf16[16,24,512]{2,1,0:T(8,128)(2,1)S(1)} %bitcast.572), channel_id=1, replica_groups=mesh['section'=2,'expert'=16,'dp'=4] {'expert'}, dimensions={0} | all-to-all | bytes 786432 | tf_op jit(solution)/shard_map/all_to_all | solution.py:170
  701.4 22.7 %all-gather.17.cloned.1.call-done = bf16[1,1536,512]{2,1,0:T(8,128)(2,1)} async-done(((bf16[1,384,512]{2,1,0:T(8,128)(2,1)}), bf16[1,1536,512]{2,1,0:T(8,128)(2,1)}) %all-gather.17.cloned.1.call-update) | async-done | bytes 1572880 | tf_op jit(solution)/shard_map/all_gather | solution.py:174
  724.1 9.8 fusion.23
  785.7 16.8 %scatter_fusion.2 = f32[150,16]{0,1:T(8,128)S(1)} fusion(f32[150,16]{0,1:T(8,128)S(1)} %broadcast_in_dim.85, s32[300]{0:T(512)S(1)} %reshape.2224, f32[300]{0:T(512)S(1)} %reshape.2226), kind=kCustom, calls=%fused_computation.20 | custom fusion | flops 300 | bytes 6000 | tf_op jit(solution)/shard_map/transpose(jvp(jit(take_along_axis)))/scatter-add | solution.py:39
  854.1 350.1 %all-reduce.6 = (f32[2,512]{1,0:T(2,128)S(1)}, f32[2,512]{1,0:T(2,128)S(1)}, f32[512,16]{1,0:T(8,128)S(1)}) all-reduce(f32[2,512]{1,0:T(2,128)S(1)} %fusion.354, f32[2,512]{1,0:T(2,128)S(1)} %fusion.355, f32[512,16]{1,0:T(8,128)S(1)} %convolution_add_fusion.10), channel_id=8, replica_groups=mesh['section'=2,'expert'=16,'dp'=4] {'expert','dp'}, use_global_device_ids=true, to_apply=%region_108.111.clone | all-reduce | flops 10240 | bytes 81920
  1206.0 183.8 %reduce-scatter.23.cloned.1.call-done = f32[8,1536]{1,0:T(8,128)} async-done(((f32[512,1536]{1,0:T(8,128)}), f32[8,1536]{1,0:T(8,128)}) %reduce-scatter.23.cloned.1.call-update) | async-done | bytes 49168 | tf_op jit(solution)/shard_map/reduce_scatter | solution.py:325
  (879 shorter events, 446.7 us)
Async XLA Ops:
  7.2 73.0 %all-gather.7.cloned.1.call-start = ((), (), s32[]{:S(2)}) async-start(), calls=%async_computation.20 | async-start | bytes 1966080 | tf_op jit(solution)/shard_map/all_gather | solution.py:261
  55.5 77.8 %reduce-scatter.11.cloned.1.call-start = ((), (), s32[]{:S(2)}) async-start(), calls=%async_computation.21 | async-start | bytes 3932160 | tf_op jit(solution)/shard_map/reduce_scatter | solution.py:269
  135.2 16.9 %all-to-all-start.1 = ((bf16[16,24,512]{2,1,0:T(8,128)(2,1)}), bf16[16,24,512]{2,1,0:T(8,128)(2,1)S(1)}, u32[]{:S(2)}, u32[]{:S(2)}) async-start(bf16[16,24,512]{2,1,0:T(8,128)(2,1)} %bitcast.580), calls=%async_computation.2 | async-start | bytes 786432 | tf_op jit(solution)/shard_map/all_to_all | solution.py:272
  142.2 75.9 %all-gather.9.cloned.1.call-start = ((), (), s32[]{:S(2)}) async-start(), calls=%async_computation.22 | async-start | bytes 1966080 | tf_op jit(solution)/shard_map/all_gather | solution.py:261
  194.9 75.3 %reduce-scatter.13.cloned.1.call-start = ((), (), s32[]{:S(2)}) async-start(), calls=%async_computation.23 | async-start | bytes 3932160 | tf_op jit(solution)/shard_map/reduce_scatter | solution.py:269
  272.1 20.1 %all-to-all-start.3 = ((bf16[16,24,512]{2,1,0:T(8,128)(2,1)}), bf16[16,24,512]{2,1,0:T(8,128)(2,1)S(1)}, u32[]{:S(2)}, u32[]{:S(2)}) async-start(bf16[16,24,512]{2,1,0:T(8,128)(2,1)} %bitcast.579), calls=%async_computation.5 | async-start | bytes 786432 | tf_op jit(solution)/shard_map/all_to_all | solution.py:272
  292.2 17.1 %all-to-all-start.6 = ((bf16[16,24,512]{2,1,0:T(8,128)(2,1)}), bf16[16,24,512]{2,1,0:T(8,128)(2,1)}, u32[]{:S(2)}, u32[]{:S(2)}) async-start(bf16[16,24,512]{2,1,0:T(8,128)(2,1)} %bitcast.566), calls=%async_computation.9 | async-start | bytes 786432 | tf_op jit(solution)/shard_map/all_to_all | solution.py:170
  299.6 50.7 %all-gather.13.cloned.1.call-start = ((), (), s32[]{:S(2)}) async-start(), calls=%async_computation.26 | async-start | bytes 1966080 | tf_op jit(solution)/shard_map/all_gather | solution.py:174
  308.0 2.5 collective-permute-start.1
  309.3 63.8 %all-gather.11.cloned.1.call-start = ((), (), s32[]{:S(2)}) async-start(), calls=%async_computation.24 | async-start | bytes 1966080 | tf_op jit(solution)/shard_map/all_gather | solution.py:261
  350.0 63.9 %reduce-scatter.17.cloned.1.call-start = ((), (), s32[]{:S(2)}) async-start(), calls=%async_computation.27 | async-start | bytes 3932160 | tf_op jit(solution)/shard_map/reduce_scatter | solution.py:189
  364.1 90.2 %reduce-scatter.15.cloned.1.call-start = ((), (), s32[]{:S(2)}) async-start(), calls=%async_computation.25 | async-start | bytes 3932160 | tf_op jit(solution)/shard_map/reduce_scatter | solution.py:269
  415.8 17.0 %all-to-all-start.7 = ((bf16[16,24,512]{2,1,0:T(8,128)(2,1)}), bf16[16,24,512]{2,1,0:T(8,128)(2,1)S(1)}, u32[]{:S(2)}, u32[]{:S(2)}) async-start(bf16[16,24,512]{2,1,0:T(8,128)(2,1)} %bitcast.59), calls=%async_computation.11 | async-start | bytes 786432 | tf_op jit(solution)/shard_map/all_to_all | solution.py:192
  456.2 16.9 %all-to-all-start.5 = ((bf16[16,24,512]{2,1,0:T(8,128)(2,1)}), bf16[16,24,512]{2,1,0:T(8,128)(2,1)S(1)}, u32[]{:S(2)}, u32[]{:S(2)}) async-start(bf16[16,24,512]{2,1,0:T(8,128)(2,1)} %bitcast.49), calls=%async_computation.8 | async-start | bytes 786432 | tf_op jit(solution)/shard_map/all_to_all | solution.py:272
  463.2 107.2 %all-gather.15.cloned.1.call-start = ((), (), s32[]{:S(2)}) async-start(), calls=%async_computation.28 | async-start | bytes 1966080 | tf_op jit(solution)/shard_map/all_gather | solution.py:174
  523.1 3.5 collective-permute-start.2
  547.3 75.4 %reduce-scatter.19.cloned.1.call-start = ((), (), s32[]{:S(2)}) async-start(), calls=%async_computation.29 | async-start | bytes 3932160 | tf_op jit(solution)/shard_map/reduce_scatter | solution.py:189
  624.6 26.4 %all-to-all-start.9 = ((bf16[16,24,512]{2,1,0:T(8,128)(2,1)}), bf16[16,24,512]{2,1,0:T(8,128)(2,1)S(1)}, u32[]{:S(2)}, u32[]{:S(2)}) async-start(bf16[16,24,512]{2,1,0:T(8,128)(2,1)} %bitcast.577), calls=%async_computation.14 | async-start | bytes 786432 | tf_op jit(solution)/shard_map/all_to_all | solution.py:192
  631.6 92.5 %all-gather.17.cloned.1.call-start = ((), (), s32[]{:S(2)}) async-start(), calls=%async_computation.30 | async-start | bytes 1966080 | tf_op jit(solution)/shard_map/all_gather | solution.py:174
  675.8 3.3 collective-permute-start.3
  701.0 75.3 %reduce-scatter.21.cloned.1.call-start = ((), (), s32[]{:S(2)}) async-start(), calls=%async_computation.31 | async-start | bytes 3932160 | tf_op jit(solution)/shard_map/reduce_scatter | solution.py:189
  778.2 24.4 %all-to-all-start.11 = ((bf16[16,24,512]{2,1,0:T(8,128)(2,1)}), bf16[16,24,512]{2,1,0:T(8,128)(2,1)S(1)}, u32[]{:S(2)}, u32[]{:S(2)}) async-start(bf16[16,24,512]{2,1,0:T(8,128)(2,1)} %bitcast.578), calls=%async_computation.17 | async-start | bytes 786432 | tf_op jit(solution)/shard_map/all_to_all | solution.py:192
  785.2 420.8 %reduce-scatter.25.cloned.1.call-start = ((), (), s32[]{:S(2)}) async-start(), calls=%async_computation.33 | async-start | bytes 1064960 | tf_op jit(solution)/shard_map/reduce_scatter | solution.py:326
  817.3 572.5 %reduce-scatter.23.cloned.1.call-start = ((), (), s32[]{:S(2)}) async-start(), calls=%async_computation.32 | async-start | bytes 3194880 | tf_op jit(solution)/shard_map/reduce_scatter | solution.py:325
  (207 other events, 3640.3 us)
Sparse Core Ops, SparseCore 0:
  55.6 24.5 all-gather.6
  94.9 38.2 reduce-scatter.10
  195.0 23.0 all-gather.8
  231.8 38.2 reduce-scatter.12
  309.5 26.4 all-gather.12
  350.1 22.9 all-gather.10
  375.6 38.2 reduce-scatter.16
  416.3 37.9 reduce-scatter.14
  547.4 22.9 all-gather.14
  584.3 38.2 reduce-scatter.18
  701.1 22.9 all-gather.16
  737.9 38.2 reduce-scatter.20
  817.4 351.9 reduce-scatter.24
  1174.8 214.9 reduce-scatter.22
where the time goes:
time: 1410 us; the launch traced here: 1400 us
  blocking collectives  434 us (31%)
  waiting for transfers between devices  429 us (30%)
  local copies, waits for them, and re-layouts  181 us (13%)
  matrix products  143 us (10%)
  other arithmetic  134 us (10%)
  starting transfers between devices  57.4 us (4%)
  between operations  18.4 us (1%)
    unnamed x1, blocking collectives  350 us
    reduce_scatter x1, waiting for transfers between devices, local(): lax.psum_scatter(qkv_total, ('expert', 'dp'), scatter_dimension=0, tiled=...  184 us
    reduce_scatter x3, waiting for transfers between devices, local(): lax.psum_scatter(term_out, 'dp', scatter_dimension=1, tiled=True)  74.6 us
    all_gather x3, waiting for transfers between devices, local(): experts_every = lax.all_gather(own_rows, 'dp', axis=1, tiled=True)  56.6 us
    scatter-add x6, other arithmetic, gate_values(): jnp.take_along_axis(jax.nn.softmax(logits, axis=-1), chosen, axis=1)  52.1 us
    all_to_all x3, blocking collectives, local(): lax.all_to_all(layer_send.reshape(owners, -1, features), 'expert', split_...  50.3 us
    reduce_scatter x3, waiting for transfers between devices, experts_backward(): lax.psum_scatter(grad_rows, 'dp', scatter_dimension=1, tiled=True)  49.4 us
    all_gather x3, waiting for transfers between devices, experts_backward(): grad_every = lax.all_gather(grad_finished, 'dp', axis=1, tiled=True)  45.4 us
  transfers between devices with their start and end apart: 25, of which 19 were waited for; matrix products, arithmetic and copies ran while one was open for 16% of the time, Pallas kernels for 0%

commit v1 on v0

v1 whole, which is shorter than its diff:
```python
from functools import partial

import jax
import jax.numpy as jnp
from jax import lax
from jax.experimental import pallas as pl
from jax.experimental.pallas import tpu as pltpu
from jax.sharding import PartitionSpec as P

HEADS = 8
HEAD_DIM = 64
SEQ = 50
ROWS = 64
EPSILON = 1e-06
MESH = pl.DeviceIdType.MESH
F32 = jnp.float32
BF16 = jnp.bfloat16
EXTRA = 128


def nn(a, b):
    return lax.dot_general(a, b, (((1,), (0,)), ((), ())), preferred_element_type=F32)


def nt(a, b):
    return lax.dot_general(a, b, (((1,), (1,)), ((), ())), preferred_element_type=F32)


def tn(a, b):
    return lax.dot_general(a, b, (((0,), (0,)), ((), ())), preferred_element_type=F32)


def iota(shape, dim):
    return lax.broadcasted_iota(jnp.int32, shape, dim)


def split_sum(values):
    high = values.astype(BF16)
    return high, (values - high.astype(F32)).astype(BF16)


def normalized(values):
    center = values - jnp.mean(values, axis=-1, keepdims=True)
    root = lax.rsqrt(jnp.mean(center * center, axis=-1, keepdims=True) + EPSILON)
    return center * root, root


def norm_back(grad, norm, root, gain):
    scaled = grad * gain
    return root * (
        scaled
        - jnp.mean(scaled, axis=-1, keepdims=True)
        - norm * jnp.mean(scaled * norm, axis=-1, keepdims=True)
    )


def gelu_parts(x):
    z = jnp.abs(x) * 0.7071067811865476
    t = 1.0 / (1.0 + 0.3275911 * z)
    poly = t * (
        0.254829592 + t * (-0.284496736 + t * (1.421413741 + t * (-1.453152027 + t * 1.061405429)))
    )
    bell = jnp.exp(-z * z)
    tail = 0.5 * poly * bell
    share = jnp.where(x >= 0.0, 1.0 - tail, tail)
    return x * share, share + x * bell * 0.3989422804014327


def kernel(
    dims,
    inputs, cotangent, gains, biases, w_qkv, w_out, w_router, w_in, w_up, routes,
    o_outs, o_grads, o_gain, o_bias, o_qkv, o_attn, o_router, o_in, o_up,
    xin, cot, rt, gn, bs, wq, wo, wr, wi, wu,
    place, bias, heads_mask, s0, s1, m0, m1, wr128,
    states, norm1, packed, probs, blended, attended, norm2, shares,
    pick0, pick1, stage_out, stage_grad,
    snd, rcv, rows_in, hidden, slope, acc, gbuf, gblend, gpacked, small,
    part, part_in, part_acc, part_dp,
    dense, dense_in, dense_acc, dense_dp, dense_out, dense_last,
    in_sem, w_send, w_recv, e_send, e_recv, f_send,
    a_send, a_recv, a_loc, o_send, o_recv, o_loc,
    g_send, g_recv, gd_send, gd_recv, d_send, d_recv, dx_send, dx_recv, dy_send, dy_recv, fin_sem,
):
    sections, experts, dps, tokens, features, cap, ffs, micro = dims
    images = tokens // SEQ
    total = images * ROWS
    slots = experts * cap
    half = features // 2
    pairs = HEADS // 2
    span = 2 * HEAD_DIM
    rows_dp = features // dps
    rows_own = rows_dp // experts
    width = dense.shape[-1]

    s = lax.axis_index("section")
    e = lax.axis_index("expert")
    d = lax.axis_index("dp")
    twin = (1 - s, e, d)

    def expert_peer(j):
        return (s, lax.rem(e + j, experts), d)

    def dp_peer(j):
        return (s, e, lax.rem(d + j, dps))

    def remote(src, dst, send, recv, device):
        return pltpu.make_async_remote_copy(
            src_ref=src, dst_ref=dst, send_sem=send, recv_sem=recv,
            device_id=device, device_id_type=MESH,
        )

    def arrived(ref, sem):
        pltpu.make_async_copy(ref, ref, sem).wait()

    def each(low, high, body):
        def step(j, carry):
            body(j)
            return carry
        lax.fori_loop(low, high, step, 0)

    barrier = pltpu.get_barrier_semaphore()
    each(1, experts, lambda j: pl.semaphore_signal(
        barrier, inc=1, device_id=expert_peer(j), device_id_type=MESH))
    each(1, dps, lambda j: pl.semaphore_signal(
        barrier, inc=1, device_id=dp_peer(j), device_id_type=MESH))
    pl.semaphore_signal(barrier, inc=1, device_id=twin, device_id_type=MESH)

    load_x = pltpu.make_async_copy(inputs.at[s], xin, in_sem.at[0])
    load_c = pltpu.make_async_copy(cotangent.at[s], cot, in_sem.at[1])
    load_x.start()
    dense_args = (
        (w_qkv, wq), (w_out, wo), (w_router, wr), (gains, gn), (biases, bs),
    )
    for i, (arg, kept) in enumerate(dense_args):
        pltpu.make_async_copy(arg.at[0], kept.at[s], w_recv.at[s, i]).start()
    pltpu.make_async_copy(routes.at[0, s], rt.at[s], w_recv.at[s, 5]).start()
    expert_args = ((w_in, wi), (w_up, wu))
    for i, (arg, kept) in enumerate(expert_args):
        pltpu.make_async_copy(arg.at[0, 0], kept.at[s, d], e_recv.at[i, s, d]).start()
    load_c.start()

    row = iota((total, tokens), 0)
    place[...] = jnp.where(
        ((row & (ROWS - 1)) < SEQ)
        & (iota((total, tokens), 1) == (row >> 6) * SEQ + (row & (ROWS - 1))),
        1.0, 0.0,
    ).astype(BF16)
    query = iota((total, total), 0)
    key = iota((total, total), 1)
    bias[...] = jnp.where(
        ((query >> 6) == (key >> 6)) & ((key & (ROWS - 1)) < SEQ), 0.0, -1e30
    )
    heads_mask[...] = jnp.where(iota((total, span), 1) < HEAD_DIM, 1.0, 0.0).astype(BF16)
    load_x.wait()
    states[0] = nn(place[...], xin[...]).astype(BF16)

    pl.semaphore_wait(barrier, experts - 1 + dps - 1 + 1)

    def dense_copy(i):
        arg, kept = dense_args[i]
        return remote(arg.at[0], kept.at[s], w_send.at[i], w_recv.at[s, i], twin)

    def route_copy():
        return remote(routes.at[0, 1 - s], rt.at[s], w_send.at[5], w_recv.at[s, 5], twin)

    def expert_twin(i):
        arg, kept = expert_args[i]
        return remote(arg.at[0, 0], kept.at[s, d], e_send.at[i, 0], e_recv.at[i, s, d], twin)

    def expert_dp(i, j):
        arg, kept = expert_args[i]
        return remote(arg.at[0, 0], kept.at[s, d], e_send.at[i, j], e_recv.at[i, s, d], dp_peer(j))

    def expert_forward(i, j):
        kept = expert_args[i][1]
        other = lax.rem(d + j, dps)
        return remote(
            kept.at[s, other], kept.at[s, other], f_send.at[i, j], e_recv.at[i, s, other], twin
        )

    def spread_experts():
        for i in range(2):
            each(1, dps, lambda j, i=i: expert_dp(i, j).start())

    for i in (3, 4, 0, 1, 2):
        dense_copy(i).start()
    route_copy().start()

    @pl.when(s == 0)
    def _():
        spread_experts()

    for i in range(2):
        expert_twin(i).start()

    def route(l):
        arrived(rt.at[l], w_recv.at[l, 5])
        named = nn(place[...], rt[l].astype(F32).astype(BF16))
        lane2 = iota((total, 2), 1)
        first = jnp.sum(jnp.where(lane2 == 0, named, 0.0), axis=1, keepdims=True)
        second = jnp.sum(jnp.where(lane2 == 1, named, 0.0), axis=1, keepdims=True)
        live = (iota((total, 1), 0) & (ROWS - 1)) < SEQ
        lane = iota((total, EXTRA), 1).astype(F32)
        hit0 = jnp.where(lane == jnp.where(live, first, -1.0), 1.0, 0.0)
        hit1 = jnp.where(lane == jnp.where(live, second, -1.0), 1.0, 0.0)
        below = jnp.where(iota((total, total), 1) < iota((total, total), 0), 1.0, 0.0).astype(BF16)
        before0 = nn(below, hit0.astype(BF16))
        before1 = nn(below, hit1.astype(BF16)) + jnp.sum(hit0, axis=0, keepdims=True)
        slot0 = first * cap + jnp.sum(hit0 * before0, axis=1, keepdims=True)
        slot1 = second * cap + jnp.sum(hit1 * before1, axis=1, keepdims=True)
        place_of = iota((total, slots), 1).astype(F32)
        s0[l] = jnp.where(place_of == jnp.where(live, slot0, -1.0), 1.0, 0.0).astype(BF16)
        s1[l] = jnp.where(place_of == jnp.where(live, slot1, -1.0), 1.0, 0.0).astype(BF16)
        m0[l] = hit0
        m1[l] = hit1

    each(0, 2, route)

    def exchange_send(phase, values):
        blocks = values.reshape(experts, cap, features)
        snd[...] = jnp.concatenate([blocks[:, :, :half], blocks[:, :, half:]], axis=1).astype(BF16)

        def start(j):
            peer = expert_peer(j)
            remote(
                snd.at[peer[1]], rcv.at[phase, e], a_send.at[j], a_recv.at[phase, j], peer
            ).start()
        each(1, experts, start)
        pltpu.make_async_copy(snd.at[e], rcv.at[phase, e], a_loc).start()

    def exchange_recv(phase):
        def finish(j):
            peer = expert_peer(j)
            source = lax.rem(e - j + experts, experts)
            copy = remote(
                snd.at[peer[1]], rcv.at[phase, source], a_send.at[j], a_recv.at[phase, j], peer
            )
            copy.wait_send()
            copy.wait_recv()
        each(1, experts, finish)
        pltpu.make_async_copy(snd.at[e], rcv.at[phase, e], a_loc).wait()
        blocks = rcv[phase].astype(F32)
        blocks = jnp.concatenate([blocks[:, :cap], blocks[:, cap:]], axis=2)
        return blocks.reshape(slots, features).astype(BF16)

    def gate_parts(l):
        p = shares[l]
        hit0, hit1 = m0[l], m1[l]
        live = (iota((total, 1), 0) & (ROWS - 1)) < SEQ
        pair = jnp.sum(p * (hit0 + hit1), axis=1, keepdims=True)
        inverse = 1.0 / jnp.where(live, pair, 1.0)
        gate0 = jnp.sum(p * hit0, axis=1, keepdims=True) * inverse
        gate1 = jnp.sum(p * hit1, axis=1, keepdims=True) * inverse
        return p, hit0, hit1, inverse, gate0, gate1

    def out_copy(kind, l, stage, dest):
        return remote(stage.at[l], dest.at[0, s], o_send.at[kind], o_recv.at[kind], twin)

    def out_keep(kind, l, stage, dest):
        return pltpu.make_async_copy(stage.at[l], dest.at[0, s], o_loc.at[kind])

    def hand_out(kind, l, stage, dest):
        @pl.when(s == l)
        def _():
            out_keep(kind, l, stage, dest).start()

        @pl.when(s != l)
        def _():
            out_copy(kind, l, stage, dest).start()

    def forward(l):
        for i, (_, kept) in enumerate(dense_args):
            arrived(kept.at[l], w_recv.at[l, i])
        spread = jnp.where(iota((experts, EXTRA), 0) == iota((experts, EXTRA), 1), 1.0, 0.0)
        wr128[l] = nn(wr[l], spread.astype(BF16)).astype(BF16)
        current = states[l].astype(F32)
        norm, _ = normalized(current)
        normed = (norm * gn[l, 0:1] + bs[l, 0:1]).astype(BF16)
        norm1[l] = normed
        packed[l] = nn(normed, wq[l]).astype(BF16)

        def attend(p):
            at = pl.multiple_of(p * span, span)
            queries = packed[l, :, pl.ds(at, span)]
            keys = packed[l, :, pl.ds(features + at, span)]
            values = packed[l, :, pl.ds(2 * features + at, span)]
            left = heads_mask[...]
            found = []
            for h in range(2):
                mask = left if h == 0 else (1.0 - left.astype(F32)).astype(BF16)
                scores = nt(queries * mask, keys) * HEAD_DIM ** (-0.5) + bias[...]
                scores = jnp.exp(scores - jnp.max(scores, axis=-1, keepdims=True))
                prob = scores * (1.0 / jnp.sum(scores, axis=-1, keepdims=True))
                probs[l, 2 * p + h] = prob
                found.append(nn(prob.astype(BF16), values))
            blended[l, :, pl.ds(at, span)] = jnp.where(
                iota((total, span), 1) < HEAD_DIM, found[0], found[1]
            ).astype(BF16)

        each(0, pairs, attend)
        middle = current + nn(blended[l], wo[l])
        attended[l] = middle
        norm, _ = normalized(middle)
        normed = (norm * gn[l, 1:2] + bs[l, 1:2]).astype(BF16)
        norm2[l] = normed
        exchange_send(4 * l, tn(s0[l] + s1[l], normed))

        logits = nn(normed, wr128[l])
        logits = jnp.where(iota((total, EXTRA), 1) < experts, logits, -1e30)
        logits = jnp.exp(logits - jnp.max(logits, axis=-1, keepdims=True))
        shares[l] = logits * (1.0 / jnp.sum(logits, axis=-1, keepdims=True))

        @pl.when(s == l)
        def _():
            for i, (_, kept) in enumerate(expert_args):
                arrived(kept.at[l, d], e_recv.at[i, l, d])

            def pass_on(j):
                other = lax.rem(d + j, dps)
                for i, (_, kept) in enumerate(expert_args):
                    arrived(kept.at[l, other], e_recv.at[i, l, other])
                    expert_forward(i, j).start()
            each(1, dps, pass_on)

        rows = exchange_recv(4 * l)
        rows_in[l] = rows

        @pl.when(s != l)
        def _():
            def get(j):
                for i, (_, kept) in enumerate(expert_args):
                    arrived(kept.at[l, j], e_recv.at[i, l, j])
            each(0, dps, get)

        @pl.when((s == 1) & (l == 0))
        def _():
            spread_experts()

        acc[...] = jnp.zeros_like(acc)

        def expert(b):
            after, dslope = gelu_parts(nn(rows_in[l], wi[l, b]))
            after = after.astype(BF16)
            hidden[l, b] = after
            slope[l, b] = dslope.astype(BF16)
            acc[...] += nn(after, wu[l, b])
        each(0, dps, expert)
        exchange_send(4 * l + 1, acc[...])
        _, _, _, _, gate0, gate1 = gate_parts(l)
        back = exchange_recv(4 * l + 1)
        picked0 = nn(s0[l], back)
        picked1 = nn(s1[l], back)
        pick0[l] = picked0.astype(BF16)
        pick1[l] = picked1.astype(BF16)
        result = (attended[l] + gate0 * picked0 + gate1 * picked1).astype(BF16)
        states[l + 1] = result
        stage_out[l] = tn(place[...], result).astype(BF16)
        hand_out(0, l, stage_out, o_outs)

    each(0, 2, forward)

    load_c.wait()
    gbuf[...] = nn(place[...], cot[...]).astype(BF16)

    def part_copy(b, k):
        return remote(part.at[b, k], part_in.at[b, k], g_send.at[b, k], g_recv.at[b, k], twin)

    def part_dp_copy(j, k):
        other = lax.rem(d + j, dps)
        return remote(
            part.at[other, k], part_dp.at[j - 1, k], gd_send.at[j, k], gd_recv.at[j, k], dp_peer(j)
        )

    def dense_twin():
        return remote(dense, dense_in, d_send, d_recv, twin)

    def dense_dp_copy(j):
        other = lax.rem(d + j, dps)
        return remote(
            dense.at[other], dense_dp.at[j - 1], dx_send.at[j], dx_recv.at[j], dp_peer(j)
        )

    def dense_pair():
        arrived(dense_in, d_recv)

        def pair_sum(j):
            other = lax.rem(d + j, dps)
            dense[other] = (dense[other].astype(F32) + dense_in[other].astype(F32)).astype(BF16)
            dense_dp_copy(j).start()
        each(1, dps, pair_sum)
        dense_acc[...] = dense[d].astype(F32) + dense_in[d].astype(F32)

    def last_copy(j, place_at):
        peer = expert_peer(j)
        return remote(
            dense_out.at[peer[1]], dense_last.at[place_at], dy_send.at[j], dy_recv.at[j], peer
        )

    def dense_dp_sum():
        def dp_sum(j):
            copy = dense_dp_copy(j)
            copy.wait_send()
            copy.wait_recv()
            dense_acc[...] += dense_dp[j - 1].astype(F32)
        each(1, dps, dp_sum)
        blocks = dense_acc[...].reshape(experts, rows_own, width)
        dense_out[...] = jnp.concatenate(
            [blocks[:, :, : width // 2], blocks[:, :, width // 2:]], axis=1
        ).astype(BF16)
        each(1, experts, lambda j: last_copy(j, e).start())

    def backward(step):
        l = 1 - step
        grad_y = gbuf[...].astype(F32)
        p, hit0, hit1, inverse, gate0, gate1 = gate_parts(l)
        exchange_send(
            4 * l + 2,
            tn(s0[l], (gate0 * grad_y).astype(BF16)) + tn(s1[l], (gate1 * grad_y).astype(BF16)),
        )
        gg0 = jnp.sum(grad_y * pick0[l].astype(F32), axis=1, keepdims=True)
        gg1 = jnp.sum(grad_y * pick1[l].astype(F32), axis=1, keepdims=True)
        mixed = gate0 * gg0 + gate1 * gg1
        q = (hit0 * (gg0 - mixed) + hit1 * (gg1 - mixed)) * inverse
        glog = p * (q - jnp.sum(p * q, axis=1, keepdims=True))
        glog_high, glog_low = split_sum(glog)
        extra = tn(norm2[l], glog_high) + tn(norm2[l], glog_low)
        from_gate = nt(glog_high, wr128[l]) + nt(glog_low, wr128[l])

        @pl.when((s == 0) & (l == 0))
        def _():
            def done(b):
                for k in range(2):
                    part_copy(b, k).wait_send()
            each(0, dps, done)

        @pl.when((s == 1) & (l == 0))
        def _():
            def done(j):
                for k in range(2):
                    part_dp_copy(j, k).wait_send()
            each(1, dps, done)

            dense_pair()

        grads = exchange_recv(4 * l + 2)
        acc[...] = jnp.zeros_like(acc)
        snd_rows = grads

        def expert(b):
            before = (nt(snd_rows, wu[l, b]) * slope[l, b].astype(F32)).astype(BF16)
            slope[l, b] = before
            acc[...] += nt(before, wi[l, b])
        each(0, dps, expert)
        exchange_send(4 * l + 3, acc[...])

        def weights(b):
            part[b, 0] = tn(rows_in[l], slope[l, b]).astype(BF16)
            part[b, 1] = tn(hidden[l, b], snd_rows).astype(BF16)

            @pl.when(s != l)
            def _():
                for k in range(2):
                    part_copy(b, k).start()
        each(0, dps, weights)

        @pl.when((s == 1) & (l == 0))
        def _():
            dense_dp_sum()

        @pl.when((s == 0) & (l == 0))
        def _():
            dense_twin().wait_send()

        back = exchange_recv(4 * l + 3)
        grad_normed = nn(s0[l] + s1[l], back) + from_gate
        norm, root = normalized(attended[l])
        small[0:1] = jnp.sum(grad_normed * norm, axis=0, keepdims=True)
        small[1:2] = jnp.sum(grad_normed, axis=0, keepdims=True)
        grad_att = grad_y + norm_back(grad_normed, norm, root, gn[l, 1:2])

        @pl.when(s == l)
        def _():
            for k in range(2):
                arrived(part_in.at[d, k], g_recv.at[d, k])
                part_acc[k] = part[d, k].astype(F32) + part_in[d, k].astype(F32)

            def add(j):
                other = lax.rem(d + j, dps)
                for k in range(2):
                    arrived(part_in.at[other, k], g_recv.at[other, k])
                    part[other, k] = (
                        part[other, k].astype(F32) + part_in[other, k].astype(F32)
                    ).astype(BF16)
                    part_dp_copy(j, k).start()
            each(1, dps, add)

        branch = grad_att.astype(BF16)
        gblend[...] = nt(branch, wo[l]).astype(BF16)

        def put(values, at):
            size = values.shape[1]
            blocks = values.reshape(experts, dps, rows_own, size)
            for b in range(dps):
                dense[b, :, pl.ds(at, size)] = (
                    blocks[:, b].reshape(rows_dp, size).astype(BF16)
                )

        put(tn(blended[l], branch), 3 * features)

        def attend(p):
            at = pl.multiple_of(p * span, span)
            queries = packed[l, :, pl.ds(at, span)]
            keys = packed[l, :, pl.ds(features + at, span)]
            values = packed[l, :, pl.ds(2 * features + at, span)]
            grad_out = gblend[:, pl.ds(at, span)]
            left = heads_mask[...]
            found = []
            for h in range(2):
                mask = left if h == 0 else (1.0 - left.astype(F32)).astype(BF16)
                prob = probs[l, 2 * p + h]
                grad_prob = nt(grad_out * mask, values)
                grad_value = tn(prob.astype(BF16), grad_out)
                grad_score = prob * (
                    grad_prob - jnp.sum(prob * grad_prob, axis=-1, keepdims=True)
                )
                grad_score = grad_score.astype(BF16)
                found.append((
                    nn(grad_score, keys) * HEAD_DIM ** (-0.5),
                    tn(grad_score, queries) * HEAD_DIM ** (-0.5),
                    grad_value,
                ))
            for i in range(3):
                gpacked[:, pl.ds(i * features + at, span)] = jnp.where(
                    iota((total, span), 1) < HEAD_DIM, found[0][i], found[1][i]
                ).astype(BF16)

        each(0, pairs, attend)
        grad_normed = nt(gpacked[...], wq[l])
        current = states[l].astype(F32)
        norm, root = normalized(current)
        small[2:3] = jnp.sum(grad_normed * norm, axis=0, keepdims=True)
        small[3:4] = jnp.sum(grad_normed, axis=0, keepdims=True)
        result = (grad_att + norm_back(grad_normed, norm, root, gn[l, 0:1])).astype(BF16)
        gbuf[...] = result
        stage_grad[l] = tn(place[...], result).astype(BF16)
        hand_out(1, l, stage_grad, o_grads)
        for i in range(3):
            put(tn(norm1[l], gpacked[:, i * features:(i + 1) * features]), i * features)
        high, low = split_sum(small[...])
        lane = iota((8, EXTRA), 1)
        line = iota((8, EXTRA), 0)
        column = jnp.where((lane == line + experts) & (line < 4), 1.0, 0.0).astype(BF16)
        put(extra + tn(high, column) + tn(low, column), 4 * features)

        @pl.when(s != l)
        def _():
            dense_twin().start()

    small[...] = jnp.zeros_like(small)
    dense[:, :, pl.ds(4 * features + EXTRA, width - 4 * features - EXTRA)] = jnp.zeros(
        (dps, rows_dp, width - 4 * features - EXTRA), BF16
    )
    each(0, 2, backward)

    @pl.when(s == 0)
    def _():
        dense_pair()
        dense_dp_sum()

    def part_sum(j):
        for k in range(2):
            arrived(part_dp.at[j - 1, k], gd_recv.at[j, k])
            part_acc[k] += part_dp[j - 1, k].astype(F32)
    each(1, dps, part_sum)
    keep_in = pltpu.make_async_copy(part_acc.at[0], o_in.at[0, 0], fin_sem.at[0])
    keep_up = pltpu.make_async_copy(part_acc.at[1], o_up.at[0, 0], fin_sem.at[1])
    keep_in.start()
    keep_up.start()

    dense_last[e] = dense_out[e]

    def last_wait(j):
        copy = last_copy(j, lax.rem(e - j + experts, experts))
        copy.wait_send()
        copy.wait_recv()
    each(1, experts, last_wait)
    final = jnp.sum(dense_last[...].astype(F32), axis=0)
    final = jnp.concatenate([final[:rows_own], final[rows_own:]], axis=1)
    o_qkv[0] = final[:, : 3 * features]
    o_attn[0] = final[:, 3 * features: 4 * features]
    tail = final[:, 4 * features: 4 * features + EXTRA]
    o_router[0] = tail[:, :experts]
    tail_high, tail_low = split_sum(tail)
    tail_low, tail_rest = split_sum(tail - tail_high.astype(F32))

    def column_rows(late, early):
        lane = iota((2, EXTRA), 1)
        line = iota((2, EXTRA), 0)
        wanted = jnp.where(line == 0, experts + early, experts + late)
        pick = jnp.where(lane == wanted, 1.0, 0.0).astype(BF16)
        return nt(pick, tail_high) + nt(pick, tail_low) + nt(pick, tail_rest)

    o_gain[0] = column_rows(0, 2)
    o_bias[0] = column_rows(1, 3)

    for i in range(5):
        dense_copy(i).wait_send()
    route_copy().wait_send()
    for i in range(2):
        expert_twin(i).wait_send()

        def spread_done(j, i=i):
            expert_dp(i, j).wait_send()
            expert_forward(i, j).wait_send()
        each(1, dps, spread_done)

    @pl.when(s == 0)
    def _():
        def done(j):
            for k in range(2):
                part_dp_copy(j, k).wait_send()
        each(1, dps, done)

    @pl.when(s == 1)
    def _():
        def done(b):
            for k in range(2):
                part_copy(b, k).wait_send()
        each(0, dps, done)
        dense_twin().wait_send()

    for kind, stage, dest in ((0, stage_out, o_outs), (1, stage_grad, o_grads)):
        out_copy(kind, 1 - s, stage, dest).wait_send()
        arrived(dest.at[0, 1 - s], o_recv.at[kind])
        out_keep(kind, s, stage, dest).wait()
    keep_in.wait()
    keep_up.wait()


def local(dims, *args):
    sections, experts, dps, tokens, features, cap, ffs, micro = dims
    total = tokens // SEQ * ROWS
    slots = experts * cap
    rows_dp = features // dps
    rows_own = rows_dp // experts
    width = -(-(4 * features + EXTRA) // 256) * 256
    half = features // 2
    block = ffs // dps
    dma = pltpu.SemaphoreType.DMA
    anywhere = pl.BlockSpec(memory_space=pl.ANY)
    vmem = pl.BlockSpec(memory_space=pltpu.VMEM)

    def out(*shape, dtype=F32):
        return jax.ShapeDtypeStruct(shape, dtype)

    out_shape = (
        out(1, micro, tokens, features, dtype=BF16),
        out(1, micro, tokens, features, dtype=BF16),
        out(1, 2, rows_own),
        out(1, 2, rows_own),
        out(1, rows_own, 3 * features),
        out(1, rows_own, features),
        out(1, rows_own, experts),
        out(1, 1, features, block),
        out(1, 1, block, features),
    )
    V = pltpu.VMEM
    scratch = [
        V((tokens, features), BF16), V((tokens, features), BF16), V((2, tokens, 2), jnp.int32),
        V((2, 2, features), F32), V((2, 2, features), F32),
        V((2, features, 3 * features), BF16), V((2, features, features), BF16),
        V((2, features, experts), BF16),
        V((2, dps, features, block), BF16), V((2, dps, block, features), BF16),
        V((total, tokens), BF16), V((total, total), F32), V((total, 2 * HEAD_DIM), BF16),
        V((2, total, slots), BF16), V((2, total, slots), BF16),
        V((2, total, EXTRA), F32), V((2, total, EXTRA), F32), V((2, features, EXTRA), BF16),
        V((3, total, features), BF16), V((2, total, features), BF16),
        V((2, total, 3 * features), BF16), V((2, HEADS, total, total), F32),
        V((2, total, features), BF16), V((2, total, features), F32),
        V((2, total, features), BF16), V((2, total, EXTRA), F32),
        V((2, total, features), BF16), V((2, total, features), BF16),
        V((2, tokens, features), BF16), V((2, tokens, features), BF16),
        V((experts, 2 * cap, half), BF16), V((8, experts, 2 * cap, half), BF16),
        V((2, slots, features), BF16),
        V((2, dps, slots, block), BF16), V((2, dps, slots, block), BF16),
        V((slots, features), F32),
        V((total, features), BF16), V((total, features), BF16), V((total, 3 * features), BF16),
        V((8, features), F32),
        V((dps, 2, features, block), BF16), V((dps, 2, features, block), BF16),
        V((2, features, block), F32), V((dps - 1, 2, features, block), BF16),
        V((dps, rows_dp, width), BF16), V((dps, rows_dp, width), BF16),
        V((rows_dp, width), F32), V((dps - 1, rows_dp, width), BF16),
        V((experts, 2 * rows_own, width // 2), BF16), V((experts, 2 * rows_own, width // 2), BF16),
        dma((2,)), dma((6,)), dma((2, 6)), dma((2, dps)), dma((2, 2, dps)), dma((2, dps)),
        dma((experts,)), dma((8, experts)), dma, dma((2,)), dma((2,)), dma((2,)),
        dma((dps, 2)), dma((dps, 2)), dma((dps, 2)), dma((dps, 2)),
        dma, dma, dma((dps,)), dma((dps,)), dma((experts,)), dma((experts,)), dma((2,)),
    ]
    return pl.pallas_call(
        partial(kernel, dims),
        out_shape=out_shape,
        in_specs=[anywhere, anywhere, vmem, vmem, anywhere, anywhere, vmem, anywhere, anywhere, vmem],
        out_specs=(anywhere, anywhere, vmem, vmem, vmem, vmem, vmem, anywhere, anywhere),
        scratch_shapes=scratch,
        compiler_params=pltpu.CompilerParams(
            collective_id=0, has_side_effects=True, vmem_limit_bytes=62 * 2**20
        ),
        cost_estimate=pl.CostEstimate(
            flops=10_000_000_000, bytes_accessed=10_000_000, transcendentals=4_000_000
        ),
    )(*args)


def solution(mesh):
    sections, experts, dps = (mesh.shape[name] for name in ("section", "expert", "dp"))

    def run(*args):
        tokens, features = args[0].shape[1:]
        micro = args[0].shape[0]
        cap = 5 * tokens // (2 * experts) + 1
        ffs = args[7].shape[3] * dps
        dims = (sections, experts, dps, tokens, features, cap, ffs, micro)
        return local(dims, *args)

    return jax.shard_map(
        run,
        mesh=mesh,
        in_specs=(
            P(None, ("expert", "dp"), None),
            P(None, ("expert", "dp"), None),
            P("section", None, None),
            P("section", None, None),
            P("section", None, None),
            P("section", None, None),
            P("section", None, None),
            P("section", "expert", None, "dp"),
            P("section", "expert", "dp", None),
            P("section", None, ("expert", "dp"), None),
        ),
        out_specs=(
            P("section", None, ("expert", "dp"), None),
            P("section", None, ("expert", "dp"), None),
            P("section", None, ("expert", "dp")),
            P("section", None, ("expert", "dp")),
            P("section", ("expert", "dp"), None),
            P("section", ("expert", "dp"), None),
            P("section", ("expert", "dp"), None),
            P("section", "expert", None, "dp"),
            P("section", "expert", "dp", None),
        ),
        check_vma=False,
    )
```

time: 1410 us -> 208 us (0.15)
  blocking collectives: 434 us -> 0 us
  waiting for transfers between devices: 429 us -> 0 us
  Pallas kernels: 0 us -> 188 us
  local copies, waits for them, and re-layouts: 181 us -> 18.7 us
  matrix products: 143 us -> 0 us
  other arithmetic: 134 us -> 0 us
  starting transfers between devices: 57.4 us -> 0 us
  between operations: 18.4 us -> 0.67 us
    unnamed x1 -> x0, blocking collectives: 350 us -> none
    reduce_scatter x8 -> x0, waiting for transfers between devices: 308 us -> none  [the longest x1 184 us: local(): lax.psum_scatter(qkv_total, ('expert', 'dp'), scatter_dimension=0, tiled=...]
    pallas_call x0 -> x1, Pallas kernels: none -> 188 us  [local(): pl.pallas_call(partial(kernel, dims), out_shape=out_shape, in_specs=[anyw...]
    dot_general x66 -> x0, matrix products: 143 us -> none  [the longest x3 29.6 us: experts_backward(): jnp.einsum('erd,efd->erf', grad_every, use_out, preferred_element_type=jn...]
    all_gather x6 -> x0, waiting for transfers between devices: 102 us -> none  [the longest x3 56.6 us: local(): experts_every = lax.all_gather(own_rows, 'dp', axis=1, tiled=True)]
    all_to_all x5 -> x0, blocking collectives: 83.7 us -> none  [the longest x3 50.3 us: local(): lax.all_to_all(layer_send.reshape(owners, -1, features), 'expert', split_...]
    scatter-add x6 -> x0, other arithmetic: 52.1 us -> none  [gate_values(): jnp.take_along_axis(jax.nn.softmax(logits, axis=-1), chosen, axis=1)]
    all_to_all x7 -> x0, starting transfers between devices: 49.8 us -> none  [the longest x3 21.4 us: local(): lax.all_to_all(source_rows(finished, owners), 'expert', split_axis=0, con...]
  transfers between devices with their start and end apart: 25 -> 0, of which waited for: 19 -> 0; matrix products, arithmetic and copies ran while one was open for 16% -> 0% of each run, Pallas kernels for 0% -> 0%
where the time goes in v1:
time: 208 us; the launch traced here: 207 us
  Pallas kernels  188 us (90%)
  local copies, waits for them, and re-layouts  18.7 us (9%)
    pallas_call x1, Pallas kernels, local(): pl.pallas_call(partial(kernel, dims), out_shape=out_shape, in_specs=[anyw...  188 us
    unnamed x15, local copies, waits for them, and re-layouts  14.7 us

profile of v1, /device:TPU:0, one launch (start us, length us, event | category | flops | bytes accessed | tf_op | source)
XLA Modules:
  0.0 207.2 jit_solution(813792988402111895)
XLA Ops:
  0.6 1.5 copy.21.w_router
  2.1 1.5 copy.22.routes
  3.6 1.7 copy.19.inputs
  5.3 1.7 copy.20.cotangent
  7.0 187.8 %shard_map.169 = (bf16[1,2,150,512]{3,2,1,0:T(8,128)(2,1)}, bf16[1,2,150,512]{3,2,1,0:T(8,128)(2,1)}, f32[1,2,8]{2,1,0:T(2,128)}, f32[1,2,8]{2,1,0:T(2,128)}, f3...) custom-call(bf16[2,150,512]{2,1,0:T(8,128)(2,1)} %copy.19.inputs, ...), custom_call_target="tpu_custom_call" | custom-call | flops 10000000000 | bytes 10000000 | tf_op jit(solution)/shard_map/pallas_call | solution.py:699
  194.8 0.0 copy-start.1
  194.8 2.0 copy.23
  196.8 0.0 copy-start
  196.8 2.0 copy.24
  198.9 1.2 copy.32
  200.0 1.2 copy.33
  201.2 1.4 copy.34
  202.6 1.3 copy.35
  204.0 1.3 copy.36
  205.2 0.0 copy-done.1
  205.2 1.0 copy.37
  206.2 0.0 copy-done
  206.2 1.0 copy.38
Async XLA Ops:
  194.8 10.4 %copy-start.1 = (f32[1,1,512,512]{3,2,1,0:T(8,128)S(1)}, f32[1,1,512,512]{3,2,1,0:T(8,128)}, u32[]{:S(2)}) copy-start(f32[1,1,512,512]{3,2,1,0:T(8,128)} %get-tuple-element.34) | copy-start | bytes 3145732
  196.8 9.4 %copy-start = (f32[1,1,512,512]{3,2,1,0:T(8,128)S(1)}, f32[1,1,512,512]{3,2,1,0:T(8,128)}, u32[]{:S(2)}) copy-start(f32[1,1,512,512]{3,2,1,0:T(8,128)} %get-tuple-element.35) | copy-start | bytes 3145732

commit v2 on v1

v2 whole, which is shorter than its diff:
```python
from functools import partial

import jax
import jax.numpy as jnp
from jax import lax
from jax.experimental import pallas as pl
from jax.experimental.pallas import tpu as pltpu
from jax.sharding import PartitionSpec as P

HEADS = 8
HEAD_DIM = 64
SEQ = 50
ROWS = 64
EPSILON = 1e-06
MESH = pl.DeviceIdType.MESH
F32 = jnp.float32
BF16 = jnp.bfloat16
EXTRA = 128
SIDE = 4
HOPS = (0, 1, 2, 1)
OFFSETS = sorted(
    ((y, z) for y in range(SIDE) for z in range(SIDE) if y or z),
    key=lambda at: -HOPS[at[0]] - HOPS[at[1]],
)


def nn(a, b):
    return lax.dot_general(a, b, (((1,), (0,)), ((), ())), preferred_element_type=F32)


def nt(a, b):
    return lax.dot_general(a, b, (((1,), (1,)), ((), ())), preferred_element_type=F32)


def tn(a, b):
    return lax.dot_general(a, b, (((0,), (0,)), ((), ())), preferred_element_type=F32)


def iota(shape, dim):
    return lax.broadcasted_iota(jnp.int32, shape, dim)


def split_sum(values):
    high = values.astype(BF16)
    return high, (values - high.astype(F32)).astype(BF16)


def normalized(values):
    center = values - jnp.mean(values, axis=-1, keepdims=True)
    root = lax.rsqrt(jnp.mean(center * center, axis=-1, keepdims=True) + EPSILON)
    return center * root, root


def norm_back(grad, norm, root, gain):
    scaled = grad * gain
    return root * (
        scaled
        - jnp.mean(scaled, axis=-1, keepdims=True)
        - norm * jnp.mean(scaled * norm, axis=-1, keepdims=True)
    )


def gelu_parts(x):
    z = jnp.abs(x) * 0.7071067811865476
    t = 1.0 / (1.0 + 0.3275911 * z)
    poly = t * (
        0.254829592 + t * (-0.284496736 + t * (1.421413741 + t * (-1.453152027 + t * 1.061405429)))
    )
    bell = jnp.exp(-z * z)
    tail = 0.5 * poly * bell
    share = jnp.where(x >= 0.0, 1.0 - tail, tail)
    return x * share, share + x * bell * 0.3989422804014327


def kernel(
    dims,
    inputs, cotangent, gains, biases, w_qkv, w_out, w_router, w_in, w_up, routes,
    o_outs, o_grads, o_norms, o_dense, o_in, o_up,
    xin, cot, rt, gn, bs, wq, wo, wr, wi, wu,
    place, s0, s1, m0, m1, wr128,
    states, norm1, packed, probs, blended, attended, norm2, shares,
    pick0, pick1, stage_out, stage_grad, join_out, join_grad,
    snd, rcv, rows_in, hidden, slope, acc, grows, gbuf, branch_kept, gblend, gpacked, small, extra_kept,
    part, part_in, part_acc, ring, ring_end,
    dense, dense_in, dense_acc, dense_dp, dense_out, dense_last,
    second, second_in, second_far, second_out, second_last,
    in_sem, w_send, w_recv, e_send, e_recv, r_send, f_send, t_send,
    a_send, a_recv, o_send, o_recv, o_loc,
    g_send, g_recv, h_send, h_recv, k_send, k_recv,
    d_send, d_recv, dx_send, dx_recv, dy_send, dy_recv, sy_send, sy_recv, sx_send, sx_recv, fin_sem,
):
    sections, experts, dps, tokens, features, cap, ffs, micro = dims
    images = tokens // SEQ
    total = images * ROWS
    slots = experts * cap
    half = features // 2
    pairs = HEADS // 2
    span = 2 * HEAD_DIM
    rows_dp = features // dps
    rows_own = rows_dp // experts
    first_width = dense.shape[-1]
    second_width = second.shape[-1]
    scale = HEAD_DIM ** (-0.5)

    s = lax.axis_index("section")
    e = lax.axis_index("expert")
    d = lax.axis_index("dp")
    e_y, e_z = e // SIDE, lax.rem(e, SIDE)
    twin = (1 - s, e, d)

    def expert_at(y, z, sign=1):
        return (
            lax.rem(e_y + SIDE + sign * y, SIDE) * SIDE + lax.rem(e_z + SIDE + sign * z, SIDE)
        )

    def around(j):
        return lax.rem(d + j, dps)

    right, left, far = around(1), around(3), around(2)
    to_right, to_left, to_far = (s, e, right), (s, e, left), (s, e, far)

    def remote(src, dst, send, recv, device):
        return pltpu.make_async_remote_copy(
            src_ref=src, dst_ref=dst, send_sem=send, recv_sem=recv,
            device_id=device, device_id_type=MESH,
        )

    def arrived(ref, sem):
        pltpu.make_async_copy(ref, ref, sem).wait()

    def each(low, high, body):
        def step(j, carry):
            body(j)
            return carry
        lax.fori_loop(low, high, step, 0)

    barrier = pltpu.get_barrier_semaphore()
    pl.semaphore_signal(barrier, inc=1, device_id=twin, device_id_type=MESH)
    for device in (to_right, to_left, to_far):
        pl.semaphore_signal(barrier, inc=1, device_id=device, device_id_type=MESH)
    for y, z in OFFSETS:
        pl.semaphore_signal(
            barrier, inc=1, device_id=(s, expert_at(y, z), d), device_id_type=MESH
        )

    load_x = pltpu.make_async_copy(inputs, xin, in_sem.at[0])
    load_c = pltpu.make_async_copy(cotangent, cot, in_sem.at[1])
    load_x.start()
    dense_args = (
        (w_qkv, wq), (w_out, wo), (w_router, wr), (gains, gn), (biases, bs),
    )
    for i, (arg, kept) in enumerate(dense_args):
        pltpu.make_async_copy(arg.at[0], kept.at[s], w_recv.at[s, i]).start()
    pltpu.make_async_copy(routes.at[0, s], rt.at[s], w_recv.at[s, 5]).start()
    expert_args = ((w_in, wi), (w_up, wu))
    for i, (arg, kept) in enumerate(expert_args):
        pltpu.make_async_copy(arg.at[0, 0], kept.at[s, d], e_recv.at[i, s, d]).start()
    load_c.start()

    row = iota((total, tokens), 0)
    place[...] = jnp.where(
        ((row & (ROWS - 1)) < SEQ)
        & (iota((total, tokens), 1) == (row >> 6) * SEQ + (row & (ROWS - 1))),
        1.0, 0.0,
    ).astype(BF16)

    def own_micro(ref):
        both = ref[...].astype(F32)
        return jnp.where(s == 0, both[:, 0, :], both[:, 1, :]).astype(BF16)

    load_x.wait()
    states[0] = nn(place[...], own_micro(xin)).astype(BF16)
    small[...] = jnp.zeros_like(small)
    spare = first_width + second_width - 4 * features - EXTRA
    second[:, pl.ds(second_width - spare, spare)] = jnp.zeros((features, spare), BF16)

    pl.semaphore_wait(barrier, 1 + 3 + len(OFFSETS))

    def dense_copy(i):
        arg, kept = dense_args[i]
        return remote(arg.at[0], kept.at[s], w_send.at[i], w_recv.at[s, i], twin)

    def route_copy():
        return remote(routes.at[0, 1 - s], rt.at[s], w_send.at[5], w_recv.at[s, 5], twin)

    def expert_twin(i):
        arg, kept = expert_args[i]
        return remote(arg.at[0, 0], kept.at[s, d], t_send.at[i], e_recv.at[i, s, d], twin)

    def expert_next(i, way):
        arg, kept = expert_args[i]
        return remote(
            arg.at[0, 0], kept.at[s, d], e_send.at[i, way], e_recv.at[i, s, d],
            (to_right, to_left)[way],
        )

    def expert_relay(way):
        kept, other = ((wi, left), (wu, right))[way]
        return remote(
            kept.at[s, other], kept.at[s, other], r_send.at[way], e_recv.at[way, s, other],
            (to_right, to_left)[way],
        )

    def expert_forward(i, j):
        kept = expert_args[i][1]
        other = around(j)
        return remote(
            kept.at[s, other], kept.at[s, other], f_send.at[i, j - 1], e_recv.at[i, s, other], twin
        )

    def spread_experts():
        for i, way in ((0, 0), (1, 1), (1, 0), (0, 1)):
            expert_next(i, way).start()

    def relay(l):
        arrived(wi.at[l, left], e_recv.at[0, l, left])
        expert_relay(0).start()
        expert_forward(0, 3).start()
        arrived(wu.at[l, right], e_recv.at[1, l, right])
        expert_relay(1).start()
        expert_forward(1, 1).start()

    def relay_rest(l):
        arrived(wi.at[l, right], e_recv.at[0, l, right])
        expert_forward(0, 1).start()
        arrived(wu.at[l, left], e_recv.at[1, l, left])
        expert_forward(1, 3).start()

    for i in (3, 4, 0, 1, 2):
        dense_copy(i).start()
    route_copy().start()

    @pl.when(s == 0)
    def _():
        spread_experts()

    for i in range(2):
        expert_twin(i).start()

    live = (iota((total, 1), 0) & (ROWS - 1)) < SEQ

    def route(l):
        arrived(rt.at[l], w_recv.at[l, 5])
        named = nt(place[...], rt[l].astype(F32).astype(BF16))
        lane2 = iota((total, 2), 1)
        first = jnp.sum(jnp.where(lane2 == 0, named, 0.0), axis=1, keepdims=True)
        second = jnp.sum(jnp.where(lane2 == 1, named, 0.0), axis=1, keepdims=True)
        lane = iota((total, EXTRA), 1).astype(F32)
        hit0 = jnp.where(lane == jnp.where(live, first, -1.0), 1.0, 0.0)
        hit1 = jnp.where(lane == jnp.where(live, second, -1.0), 1.0, 0.0)
        below = jnp.where(iota((total, total), 1) < iota((total, total), 0), 1.0, 0.0).astype(BF16)
        before0 = nn(below, hit0.astype(BF16))
        before1 = nn(below, hit1.astype(BF16)) + jnp.sum(hit0, axis=0, keepdims=True)
        slot0 = first * cap + jnp.sum(hit0 * before0, axis=1, keepdims=True)
        slot1 = second * cap + jnp.sum(hit1 * before1, axis=1, keepdims=True)
        place_of = iota((total, slots), 1).astype(F32)
        s0[l] = jnp.where(place_of == jnp.where(live, slot0, -1.0), 1.0, 0.0).astype(BF16)
        s1[l] = jnp.where(place_of == jnp.where(live, slot1, -1.0), 1.0, 0.0).astype(BF16)
        m0[l] = hit0
        m1[l] = hit1

    def exchange_send(phase, way, values):
        blocks = values.reshape(experts, cap, features)
        snd[way] = jnp.concatenate(
            [blocks[:, :, :half], blocks[:, :, half:]], axis=1
        ).astype(BF16)
        for y, z in OFFSETS:
            peer = expert_at(y, z)
            remote(
                snd.at[way, peer], rcv.at[phase, e], a_send.at[way], a_recv.at[phase], (s, peer, d)
            ).start()
        pltpu.make_async_copy(snd.at[way, e], rcv.at[phase, e], a_recv.at[phase]).start()

    def exchange_recv(phase, way):
        arrived(rcv.at[phase], a_recv.at[phase])
        sent = snd.at[way, pl.ds(0, experts - 1)]
        arrived(sent, a_send.at[way])
        blocks = rcv[phase].astype(F32)
        blocks = jnp.concatenate([blocks[:, :cap], blocks[:, cap:]], axis=2)
        return blocks.reshape(slots, features).astype(BF16)

    def gate_parts(l):
        p = shares[l]
        hit0, hit1 = m0[l], m1[l]
        pair = jnp.sum(p * (hit0 + hit1), axis=1, keepdims=True)
        inverse = 1.0 / jnp.where(live, pair, 1.0)
        gate0 = jnp.sum(p * hit0, axis=1, keepdims=True) * inverse
        gate1 = jnp.sum(p * hit1, axis=1, keepdims=True) * inverse
        return p, hit0, hit1, inverse, gate0, gate1

    def out_copy(kind, l, stage):
        return remote(
            stage.at[l], (stage_out, stage_grad)[kind].at[2], o_send.at[kind], o_recv.at[kind], twin
        )

    def hand_out(kind, l, stage, values):
        stage[l] = tn(place[...], values).astype(BF16)

        @pl.when(s != l)
        def _():
            out_copy(kind, l, stage).start()

    def join(kind, stage, joined, dest):
        arrived(stage.at[2], o_recv.at[kind])
        own = stage[s].astype(F32)
        other = stage[2].astype(F32)
        joined[...] = jnp.stack(
            [jnp.where(s == 0, own, other), jnp.where(s == 0, other, own)], axis=1
        ).astype(BF16)
        return pltpu.make_async_copy(joined, dest, o_loc.at[kind])

    def pair_keys(ref_rows, side):
        return jnp.concatenate([ref_rows * side, ref_rows * (1.0 - side)], axis=0).astype(BF16)

    lane_side = jnp.where(iota((1, span), 1) < HEAD_DIM, 1.0, 0.0)
    in_left = iota((total, span), 1) < HEAD_DIM

    def attention(l):
        for i, (_, kept) in enumerate(dense_args):
            arrived(kept.at[l], w_recv.at[l, i])
        current = states[l].astype(F32)
        norm, _ = normalized(current)
        normed = (norm * gn[l, 0:1] + bs[l, 0:1]).astype(BF16)
        norm1[l] = normed
        packed[l] = nn(normed, wq[l]).astype(BF16)
        key_bias = jnp.where((iota((1, span), 1) & (ROWS - 1)) < SEQ, 0.0, -1e30)
        for p in range(pairs):
            at = p * span
            scores = jnp.concatenate([
                nt(
                    packed[l, i * ROWS:(i + 1) * ROWS, at:at + span],
                    pair_keys(packed[
                        l, i * ROWS:(i + 1) * ROWS, features + at:features + at + span
                    ].astype(F32), lane_side),
                )
                for i in range(images)
            ], axis=0) * scale + key_bias
            top0 = jnp.max(jnp.where(in_left, scores, -1e30), axis=-1, keepdims=True)
            top1 = jnp.max(jnp.where(in_left, -1e30, scores), axis=-1, keepdims=True)
            powers = jnp.exp(scores - jnp.where(in_left, top0, top1))
            sum0 = jnp.sum(jnp.where(in_left, powers, 0.0), axis=-1, keepdims=True)
            sum1 = jnp.sum(jnp.where(in_left, 0.0, powers), axis=-1, keepdims=True)
            prob = powers * jnp.where(in_left, 1.0 / sum0, 1.0 / sum1)
            probs[l, p] = prob
            low = prob.astype(BF16)
            for i in range(images):
                values = packed[
                    l, i * ROWS:(i + 1) * ROWS, 2 * features + at:2 * features + at + span
                ].astype(F32)
                blended[l, i * ROWS:(i + 1) * ROWS, at:at + span] = nn(
                    low[i * ROWS:(i + 1) * ROWS], pair_keys(values, lane_side)
                ).astype(BF16)
        middle = current + nn(blended[l], wo[l])
        attended[l] = middle
        norm, _ = normalized(middle)
        normed = (norm * gn[l, 1:2] + bs[l, 1:2]).astype(BF16)
        norm2[l] = normed
        exchange_send(4 * l, 0, tn(s0[l] + s1[l], normed))
        spread = jnp.where(iota((EXTRA, experts), 0) == iota((EXTRA, experts), 1), 1.0, 0.0)
        wr128[l] = nn(spread.astype(BF16), wr[l]).astype(BF16)
        logits = nt(normed, wr128[l])
        logits = jnp.where(iota((total, EXTRA), 1) < experts, logits, -1e30)
        logits = jnp.exp(logits - jnp.max(logits, axis=-1, keepdims=True))
        shares[l] = logits * (1.0 / jnp.sum(logits, axis=-1, keepdims=True))

    def block_at(step):
        return around(step + step // 2 - 2 * (step // 3))

    def expert_forward_pass(l):
        rows_in[l] = exchange_recv(4 * l, 0)
        acc[...] = jnp.zeros_like(acc)

        def block(step):
            b = block_at(step)

            @pl.when((s == l) & (step == 0))
            def _():
                for i, (_, kept) in enumerate(expert_args):
                    arrived(kept.at[l, d], e_recv.at[i, l, d])

            @pl.when((s == l) & (step == 3))
            def _():
                for i, (_, kept) in enumerate(expert_args):
                    arrived(kept.at[l, far], e_recv.at[i, l, far])
                    expert_forward(i, 2).start()

            @pl.when(s != l)
            def _():
                for i, (_, kept) in enumerate(expert_args):
                    arrived(kept.at[l, b], e_recv.at[i, l, b])

            after, dslope = gelu_parts(nn(rows_in[l], wi[l, b]))
            after = after.astype(BF16)
            hidden[l, b] = after
            slope[l, b] = dslope.astype(BF16)
            acc[...] += nn(after, wu[l, b])
        each(0, dps, block)
        exchange_send(4 * l + 1, 0, acc[...])

    def slot_grads(l, way, grad_y, gate0, gate1):
        exchange_send(
            4 * l + 2, way,
            tn(s0[l], (gate0 * grad_y).astype(BF16)) + tn(s1[l], (gate1 * grad_y).astype(BF16)),
        )

    def expert_backward_pass(l, way):
        grows[...] = exchange_recv(4 * l + 2, way)
        acc[...] = jnp.zeros_like(acc)

        def block(b):
            before = (nt(grows[...], wu[l, b]) * slope[l, b].astype(F32)).astype(BF16)
            slope[l, b] = before
            acc[...] += nt(before, wi[l, b])
        each(0, dps, block)
        exchange_send(4 * l + 3, way, acc[...])

    def part_copy(b, k):
        return remote(part.at[b, k], part_in.at[b, k], g_send.at[b, k], g_recv.at[b, k], twin)

    def expert_weights(l):
        def block(step):
            b = around(2 + step)
            part[b, 0] = tn(rows_in[l], slope[l, b]).astype(BF16)

            @pl.when(s != l)
            def _():
                part_copy(b, 0).start()

            part[b, 1] = tn(hidden[l, b], grows[...]).astype(BF16)

            @pl.when(s != l)
            def _():
                part_copy(b, 1).start()
        each(0, dps, block)

    def pair_part(b, k):
        arrived(part_in.at[b, k], g_recv.at[b, k])
        return part[b, k].astype(F32) + part_in[b, k].astype(F32)

    def ring_copy(k):
        return remote(
            part.at[far, k], ring.at[k], h_send.at[k], h_recv.at[k], (to_right, to_left)[k]
        )

    def ring_last(way, k):
        return remote(
            part.at[(right, left)[way], k], ring_end.at[way, k], k_send.at[way, k],
            k_recv.at[way, k], (to_right, to_left)[way],
        )

    def ring_first_step():
        for k in range(2):
            part[far, k] = pair_part(far, k).astype(BF16)
            ring_copy(k).start()

    def ring_second_step():
        for way, k in ((0, 1), (1, 0), (0, 0), (1, 1)):
            b = (right, left)[way]
            value = pair_part(b, k)
            if way == k:
                arrived(ring.at[k], h_recv.at[k])
                value = value + ring[k].astype(F32)
            part[b, k] = value.astype(BF16)
            ring_last(way, k).start()
        for k in range(2):
            part_acc[k] = pair_part(d, k)

    def ring_sent():
        for k in range(2):
            ring_copy(k).wait_send()
            for way in range(2):
                ring_last(way, k).wait_send()

    def part_sent():
        def done(b):
            for k in range(2):
                part_copy(b, k).wait_send()
        each(0, dps, done)

    def dense_twin(b):
        return remote(dense.at[b], dense_in.at[b], d_send.at[b], d_recv.at[b], twin)

    def dense_dp_copy(j):
        return remote(
            dense.at[around(j)], dense_dp.at[j - 1], dx_send.at[j - 1], dx_recv.at[j - 1],
            (s, e, around(j)),
        )

    def second_twin():
        return remote(second, second_in, d_send.at[dps], d_recv.at[dps], twin)

    def second_dp_copy(j):
        return remote(
            second_out.at[around(j)], second_last.at[d], sx_send.at[j - 1], sx_recv,
            (s, e, around(j)),
        )

    def narrow(values):
        half_width = values.shape[-1] // 2
        return jnp.concatenate(
            [values[:, :, :half_width], values[:, :, half_width:]], axis=1
        ).astype(BF16)

    def widen(values):
        return jnp.concatenate([values[:rows_own], values[rows_own:]], axis=1)

    def dense_pair():
        arrived(second_in, d_recv.at[dps])
        rows = rows_own * dps

        def pair(j):
            at = pl.ds(pl.multiple_of(j * rows, rows), rows)
            second[at] = (second[at].astype(F32) + second_in[at].astype(F32)).astype(BF16)
        each(0, experts, pair)
        for y, z in OFFSETS:
            peer = expert_at(y, z)
            at = pl.ds(pl.multiple_of(peer * rows, rows), rows)
            remote(second.at[at], second_far.at[e], sy_send, sy_recv, (s, peer, d)).start()
        at = pl.ds(pl.multiple_of(e * rows, rows), rows)
        pltpu.make_async_copy(second.at[at], second_far.at[e], sy_recv).start()
        for j in (2, 1, 3):
            other = around(j)
            arrived(dense_in.at[other], d_recv.at[other])
            dense[other] = (dense[other].astype(F32) + dense_in[other].astype(F32)).astype(BF16)
            dense_dp_copy(j).start()
        arrived(dense_in.at[d], d_recv.at[d])
        dense_acc[...] = dense[d].astype(F32) + dense_in[d].astype(F32)

    def dense_middle():
        arrived(second_far, sy_recv)
        arrived(second.at[pl.ds(0, features - rows_own * dps)], sy_send)
        summed = second_far[0].astype(F32)
        for j in range(1, experts):
            summed = summed + second_far[j].astype(F32)
        second_out[...] = narrow(summed.reshape(dps, rows_own, second_width))
        for j in (2, 1, 3):
            second_dp_copy(j).start()
        pltpu.make_async_copy(second_out.at[d], second_last.at[d], sx_recv).start()
        for j in (1, 3, 2):
            copy = dense_dp_copy(j)
            copy.wait_send()
            copy.wait_recv()
        summed = dense_acc[...]
        for j in range(dps - 1):
            summed = summed + dense_dp[j].astype(F32)
        dense_out[...] = narrow(summed.reshape(experts, rows_own, first_width))
        for y, z in OFFSETS:
            peer = expert_at(y, z)
            remote(
                dense_out.at[peer], dense_last.at[e], dy_send, dy_recv, (s, peer, d)
            ).start()
        pltpu.make_async_copy(dense_out.at[e], dense_last.at[e], dy_recv).start()

    def put(values, at):
        size = values.shape[1]
        if at >= first_width:
            second[:, pl.ds(at - first_width, size)] = values.astype(BF16)
            return
        if at + size > first_width:
            put(values[:, first_width - at:], first_width)
            values = values[:, :first_width - at]
            size = first_width - at
        blocks = values.reshape(experts, dps, rows_own, size)
        for b in range(dps):
            dense[b, :, pl.ds(at, size)] = blocks[:, b].reshape(rows_dp, size).astype(BF16)

    def put_extra(l):
        high, low = split_sum(small[l])
        lane = iota((8, EXTRA), 1)
        line = iota((8, EXTRA), 0)
        column = jnp.where((lane == line + experts) & (line < 4), 1.0, 0.0).astype(BF16)
        put(extra_kept[l] + tn(high, column) + tn(low, column), 4 * features)

    def put_dense(l):
        put(tn(blended[l], branch_kept[...]), 3 * features)
        put_extra(l)
        for i in (2, 1):
            put(tn(norm1[l], gpacked[:, i * features:(i + 1) * features]), i * features)

        @pl.when(s != l)
        def _():
            second_twin().start()

        put(tn(norm1[l], gpacked[:, :features]), 0)

        @pl.when(s != l)
        def _():
            for j in (2, 1, 3, 0):
                dense_twin(around(j)).start()

    def dense_twin_sent():
        second_twin().wait_send()
        for b in range(dps):
            dense_twin(b).wait_send()

    def gate_back(l, grad_y, gates):
        p, hit0, hit1, inverse, gate0, gate1 = gates
        gg0 = jnp.sum(grad_y * pick0[l].astype(F32), axis=1, keepdims=True)
        gg1 = jnp.sum(grad_y * pick1[l].astype(F32), axis=1, keepdims=True)
        mixed = gate0 * gg0 + gate1 * gg1
        q = (hit0 * (gg0 - mixed) + hit1 * (gg1 - mixed)) * inverse
        glog = p * (q - jnp.sum(p * q, axis=1, keepdims=True))
        high, low = split_sum(glog)
        extra_kept[l] = tn(norm2[l], high) + tn(norm2[l], low)
        return nn(high, wr128[l]) + nn(low, wr128[l])

    def attention_back(l, way, grad_y, from_gate, between):
        back = exchange_recv(4 * l + 3, way)
        grad_normed = nn(s0[l] + s1[l], back) + from_gate
        norm, root = normalized(attended[l])
        small[l, 0:1] = jnp.sum(grad_normed * norm, axis=0, keepdims=True)
        small[l, 1:2] = jnp.sum(grad_normed, axis=0, keepdims=True)
        grad_att = grad_y + norm_back(grad_normed, norm, root, gn[l, 1:2])
        branch = grad_att.astype(BF16)
        branch_kept[...] = branch
        gblend[...] = nt(branch, wo[l]).astype(BF16)
        for p in range(pairs):
            at = p * span
            queries = packed[l, :, at:at + span]
            keys = packed[l, :, features + at:features + at + span]
            values = packed[l, :, 2 * features + at:2 * features + at + span]
            prob = probs[l, p]
            low = prob.astype(BF16)
            grad_prob = jnp.concatenate([
                nt(
                    gblend[i * ROWS:(i + 1) * ROWS, at:at + span],
                    pair_keys(values[i * ROWS:(i + 1) * ROWS].astype(F32), lane_side),
                )
                for i in range(images)
            ], axis=0)
            mixed = prob * grad_prob
            sum0 = jnp.sum(jnp.where(in_left, mixed, 0.0), axis=-1, keepdims=True)
            sum1 = jnp.sum(jnp.where(in_left, 0.0, mixed), axis=-1, keepdims=True)
            grad_score = (prob * (grad_prob - jnp.where(in_left, sum0, sum1))).astype(BF16)
            for i in range(images):
                rows = slice(i * ROWS, (i + 1) * ROWS)
                one = grad_score[rows]
                grad_query = nn(one, pair_keys(keys[rows].astype(F32), lane_side)) * scale
                grad_key = tn(one, queries[rows]) * scale
                grad_value = tn(low[rows], gblend[rows, at:at + span])
                side = in_left[:ROWS]
                grad_key = jnp.where(side, grad_key[:ROWS], grad_key[ROWS:])
                grad_value = jnp.where(side, grad_value[:ROWS], grad_value[ROWS:])
                gpacked[rows, at:at + span] = grad_query.astype(BF16)
                gpacked[rows, features + at:features + at + span] = grad_key.astype(BF16)
                gpacked[rows, 2 * features + at:2 * features + at + span] = grad_value.astype(BF16)
        between()
        grad_normed = nt(gpacked[...], wq[l])
        norm, root = normalized(states[l].astype(F32))
        small[l, 2:3] = jnp.sum(grad_normed * norm, axis=0, keepdims=True)
        small[l, 3:4] = jnp.sum(grad_normed, axis=0, keepdims=True)
        return grad_att, grad_normed, norm, root

    def finish_back(l, grad_att, grad_normed, norm, root):
        gbuf[...] = (grad_att + norm_back(grad_normed, norm, root, gn[l, 0:1])).astype(BF16)

    def combine(l, gate0, gate1, way):
        back = exchange_recv(4 * l + 1, way)
        picked0 = nn(s0[l], back)
        picked1 = nn(s1[l], back)
        pick0[l] = picked0.astype(BF16)
        pick1[l] = picked1.astype(BF16)
        states[l + 1] = (attended[l] + gate0 * picked0 + gate1 * picked1).astype(BF16)

    route(0)
    attention(0)

    @pl.when(s == 0)
    def _():
        relay(0)
        relay_rest(0)

    route(1)
    expert_forward_pass(0)

    @pl.when(s == 1)
    def _():
        spread_experts()

    load_c.wait()
    gbuf[...] = nn(place[...], own_micro(cot)).astype(BF16)
    gates = gate_parts(0)
    combine(0, gates[4], gates[5], 0)

    @pl.when(s == 1)
    def _():
        relay(1)

    attention(1)
    gates = gate_parts(1)
    grad_y = gbuf[...].astype(F32)
    slot_grads(1, 1, grad_y, gates[4], gates[5])

    @pl.when(s == 1)
    def _():
        relay_rest(1)

    hand_out(0, 0, stage_out, states[1])
    expert_forward_pass(1)
    expert_backward_pass(1, 1)
    expert_weights(1)
    combine(1, gates[4], gates[5], 0)
    from_gate = gate_back(1, grad_y, gates)

    @pl.when(s == 1)
    def _():
        ring_first_step()

    kept = attention_back(1, 1, grad_y, from_gate, lambda: None)
    finish_back(1, *kept)

    gates = gate_parts(0)
    grad_y = gbuf[...].astype(F32)
    slot_grads(0, 0, grad_y, gates[4], gates[5])
    put_dense(1)

    @pl.when(s == 1)
    def _():
        ring_second_step()

    hand_out(0, 1, stage_out, states[2])
    hand_out(1, 1, stage_grad, gbuf[...])
    from_gate = gate_back(0, grad_y, gates)
    expert_backward_pass(0, 0)

    @pl.when(s == 0)
    def _():
        part_sent()

    @pl.when(s == 1)
    def _():
        ring_sent()

    expert_weights(0)

    @pl.when(s == 0)
    def _():
        ring_first_step()

    @pl.when(s == 1)
    def _():
        dense_pair()

    def between():
        @pl.when(s == 0)
        def _():
            ring_second_step()
            dense_twin_sent()

        @pl.when(s == 1)
        def _():
            dense_middle()

    kept = attention_back(0, 0, grad_y, from_gate, between)
    put_dense(0)
    finish_back(0, *kept)
    hand_out(1, 0, stage_grad, gbuf[...])
    keep_out = join(0, stage_out, join_out, o_outs)
    keep_out.start()

    @pl.when(s == 0)
    def _():
        dense_pair()
        dense_middle()

    for k in range(2):
        for way in range(2):
            arrived(ring_end.at[way, k], k_recv.at[way, k])
            part_acc[k] += ring_end[way, k].astype(F32)
    keep_in = pltpu.make_async_copy(part_acc.at[0], o_in, fin_sem.at[0])
    keep_up = pltpu.make_async_copy(part_acc.at[1], o_up, fin_sem.at[1])
    keep_in.start()
    keep_up.start()
    keep_grad = join(1, stage_grad, join_grad, o_grads)
    keep_grad.start()

    arrived(dense_last, dy_recv)
    arrived(second_last, sx_recv)
    final = jnp.concatenate([
        widen(jnp.sum(dense_last[...].astype(F32), axis=0)),
        widen(jnp.sum(second_last[...].astype(F32), axis=0)),
    ], axis=1)
    o_dense[...] = final
    tail = final[:, 4 * features: 4 * features + EXTRA]
    tail_high, tail_low = split_sum(tail)
    tail_low, tail_rest = split_sum(tail - tail_high.astype(F32))

    def column_rows(late, early):
        lane = iota((2, EXTRA), 1)
        line = iota((2, EXTRA), 0)
        wanted = jnp.where(line == 0, experts + early, experts + late)
        pick = jnp.where(lane == wanted, 1.0, 0.0).astype(BF16)
        return nt(pick, tail_high) + nt(pick, tail_low) + nt(pick, tail_rest)

    o_norms[0] = column_rows(0, 2)
    o_norms[1] = column_rows(1, 3)

    for i in range(5):
        dense_copy(i).wait_send()
    route_copy().wait_send()
    for i in range(2):
        expert_twin(i).wait_send()
        expert_relay(i).wait_send()
        for way in range(2):
            expert_next(i, way).wait_send()
        for j in range(1, dps):
            expert_forward(i, j).wait_send()

    @pl.when(s == 0)
    def _():
        ring_sent()

    @pl.when(s == 1)
    def _():
        part_sent()
        dense_twin_sent()

    out_copy(0, 1 - s, stage_out).wait_send()
    out_copy(1, 1 - s, stage_grad).wait_send()
    arrived(dense_out.at[pl.ds(0, experts - 1)], dy_send)
    for j in range(1, dps):
        second_dp_copy(j).wait_send()
    keep_out.wait()
    keep_grad.wait()
    keep_in.wait()
    keep_up.wait()


def finish(
    features, outs, grads, norms, dense, part_in, part_up,
    o_outs, o_grads, o_gain, o_bias, o_qkv, o_attn, o_router, o_in, o_up,
    v_in, v_up, v_outs, v_grads, sems,
):
    passes = (
        (part_in, v_in, o_in.at[0, 0]), (part_up, v_up, o_up.at[0, 0]),
        (outs, v_outs, o_outs), (grads, v_grads, o_grads),
    )
    loads = [
        pltpu.make_async_copy(source, kept, sems.at[0, i])
        for i, (source, kept, _) in enumerate(passes)
    ]
    copies = [
        pltpu.make_async_copy(kept, dest, sems.at[1, i])
        for i, (_, kept, dest) in enumerate(passes)
    ]
    for load in loads:
        load.start()
    o_gain[0] = norms[0]
    o_bias[0] = norms[1]
    o_qkv[0] = dense[:, : 3 * features]
    o_attn[0] = dense[:, 3 * features: 4 * features]
    o_router[0] = dense[:, 4 * features: 4 * features + o_router.shape[-1]]
    for load, copy in zip(loads, copies):
        load.wait()
        copy.start()
    for copy in copies:
        copy.wait()


def local(
    dims, inputs, cotangent, gains, biases, w_qkv, w_out, w_router, w_in, w_up, routes
):
    sections, experts, dps, tokens, features, cap, ffs, micro = dims
    images = tokens // SEQ
    total = images * ROWS
    slots = experts * cap
    rows_dp = features // dps
    rows_own = rows_dp // experts
    width = -(-(4 * features + EXTRA) // 256) * 256
    first = width // 3
    second = width - first
    half = features // 2
    block = ffs // dps
    dma = pltpu.SemaphoreType.DMA
    anywhere = pl.BlockSpec(memory_space=pl.ANY)
    vmem = pl.BlockSpec(memory_space=pltpu.VMEM)

    def out(*shape, dtype=F32):
        return jax.ShapeDtypeStruct(shape, dtype)

    V = pltpu.VMEM
    pairs, span = HEADS // 2, 2 * HEAD_DIM
    scratch = [
        V((tokens, 2, features), BF16), V((tokens, 2, features), BF16),
        V((2, 2, tokens), jnp.int32),
        V((2, 2, features), F32), V((2, 2, features), F32),
        V((2, features, 3 * features), BF16), V((2, features, features), BF16),
        V((2, experts, features), BF16),
        V((2, dps, features, block), BF16), V((2, dps, block, features), BF16),
        V((total, tokens), BF16),
        V((2, total, slots), BF16), V((2, total, slots), BF16),
        V((2, total, EXTRA), F32), V((2, total, EXTRA), F32), V((2, EXTRA, features), BF16),
        V((3, total, features), BF16), V((2, total, features), BF16),
        V((2, total, 3 * features), BF16), V((2, pairs, total, span), F32),
        V((2, total, features), BF16), V((2, total, features), F32),
        V((2, total, features), BF16), V((2, total, EXTRA), F32),
        V((2, total, features), BF16), V((2, total, features), BF16),
        V((3, tokens, features), BF16), V((3, tokens, features), BF16),
        V((tokens, 2, features), BF16), V((tokens, 2, features), BF16),
        V((2, experts, 2 * cap, half), BF16), V((8, experts, 2 * cap, half), BF16),
        V((2, slots, features), BF16),
        V((2, dps, slots, block), BF16), V((2, dps, slots, block), BF16),
        V((slots, features), F32), V((slots, features), BF16),
        V((total, features), BF16), V((total, features), BF16), V((total, features), BF16),
        V((total, 3 * features), BF16),
        V((2, 8, features), F32), V((2, features, EXTRA), F32),
        V((dps, 2, features, block), BF16), V((dps, 2, features, block), BF16),
        V((2, features, block), F32), V((2, features, block), BF16),
        V((2, 2, features, block), BF16),
        V((dps, rows_dp, first), BF16), V((dps, rows_dp, first), BF16),
        V((rows_dp, first), F32), V((dps - 1, rows_dp, first), BF16),
        V((experts, 2 * rows_own, first // 2), BF16), V((experts, 2 * rows_own, first // 2), BF16),
        V((features, second), BF16), V((features, second), BF16),
        V((experts, dps * rows_own, second), BF16),
        V((dps, 2 * rows_own, second // 2), BF16), V((dps, 2 * rows_own, second // 2), BF16),
        dma((2,)), dma((6,)), dma((2, 6)), dma((2, 2)), dma((2, 2, dps)), dma((2,)),
        dma((2, dps - 1)), dma((2,)),
        dma((2,)), dma((8,)), dma((2,)), dma((2,)), dma((2,)),
        dma((dps, 2)), dma((dps, 2)), dma((2,)), dma((2,)), dma((2, 2)), dma((2, 2)),
        dma((dps + 1,)), dma((dps + 1,)), dma((dps - 1,)), dma((dps - 1,)), dma, dma, dma, dma,
        dma((dps - 1,)), dma, dma((2,)),
    ]
    made = pl.pallas_call(
        partial(kernel, dims),
        out_shape=(
            out(tokens, micro, features, dtype=BF16),
            out(tokens, micro, features, dtype=BF16),
            out(2, 2, rows_own),
            out(rows_own, width),
            out(features, block),
            out(block, features),
        ),
        in_specs=[anywhere, anywhere, vmem, vmem, anywhere, anywhere, vmem, anywhere, anywhere, vmem],
        out_specs=(anywhere, anywhere, vmem, vmem, anywhere, anywhere),
        scratch_shapes=scratch,
        compiler_params=pltpu.CompilerParams(
            collective_id=0, has_side_effects=True, vmem_limit_bytes=62 * 2**20
        ),
        cost_estimate=pl.CostEstimate(
            flops=10_000_000_000, bytes_accessed=10_000_000, transcendentals=4_000_000
        ),
    )(
        inputs.transpose(1, 0, 2), cotangent.transpose(1, 0, 2), gains, biases, w_qkv, w_out,
        w_router.transpose(0, 2, 1), w_in, w_up, routes.transpose(0, 1, 3, 2),
    )
    outs, grads, *rest = pl.pallas_call(
        partial(finish, features),
        out_shape=(
            out(tokens, micro, features, dtype=BF16),
            out(tokens, micro, features, dtype=BF16),
            out(1, 2, rows_own),
            out(1, 2, rows_own),
            out(1, rows_own, 3 * features),
            out(1, rows_own, features),
            out(1, rows_own, experts),
            out(1, 1, features, block),
            out(1, 1, block, features),
        ),
        in_specs=[anywhere, anywhere, vmem, vmem, anywhere, anywhere],
        out_specs=(anywhere, anywhere, vmem, vmem, vmem, vmem, vmem, anywhere, anywhere),
        scratch_shapes=[
            V((features, block), F32), V((block, features), F32),
            V((tokens, micro, features), BF16), V((tokens, micro, features), BF16), dma((2, 4)),
        ],
    )(*made)
    return (
        outs.transpose(1, 0, 2)[None],
        grads.transpose(1, 0, 2)[None],
        *rest,
    )


def solution(mesh):
    sections, experts, dps = (mesh.shape[name] for name in ("section", "expert", "dp"))

    def run(*args):
        tokens, features = args[0].shape[1:]
        micro = args[0].shape[0]
        cap = 5 * tokens // (2 * experts) + 1
        ffs = args[7].shape[3] * dps
        dims = (sections, experts, dps, tokens, features, cap, ffs, micro)
        return local(dims, *args)

    return jax.shard_map(
        run,
        mesh=mesh,
        in_specs=(
            P(None, ("expert", "dp"), None),
            P(None, ("expert", "dp"), None),
            P("section", None, None),
            P("section", None, None),
            P("section", None, None),
            P("section", None, None),
            P("section", None, None),
            P("section", "expert", None, "dp"),
            P("section", "expert", "dp", None),
            P("section", None, ("expert", "dp"), None),
        ),
        out_specs=(
            P("section", None, ("expert", "dp"), None),
            P("section", None, ("expert", "dp"), None),
            P("section", None, ("expert", "dp")),
            P("section", None, ("expert", "dp")),
            P("section", ("expert", "dp"), None),
            P("section", ("expert", "dp"), None),
            P("section", ("expert", "dp"), None),
            P("section", "expert", None, "dp"),
            P("section", "expert", "dp", None),
        ),
        check_vma=False,
    )
```

time: 208 us -> 126 us (0.61)
  Pallas kernels: 188 us -> 125 us
  local copies, waits for them, and re-layouts: 18.7 us -> 0 us
    pallas_call x1 -> x2, Pallas kernels: 188 us -> 125 us  [the longest x1 121 us: local(): pl.pallas_call(partial(kernel, dims), out_shape=(out(tokens, micro, featu...]
    unnamed x15 -> x0, local copies, waits for them, and re-layouts: 14.7 us -> none
    pallas_call x2 -> x0, local copies, waits for them, and re-layouts: 4.02 us -> none  [local(): pl.pallas_call(partial(kernel, dims), out_shape=out_shape, in_specs=[anyw...]
where the time goes in v2:
time: 126 us
  Pallas kernels  125 us (99%)
    pallas_call x1, Pallas kernels, local(): pl.pallas_call(partial(kernel, dims), out_shape=(out(tokens, micro, featu...  121 us
    pallas_call x1, Pallas kernels, local(): pl.pallas_call(partial(finish, features), out_shape=(out(tokens, micro, f...  4.33 us

profile of v2, /device:TPU:0, one launch (start us, length us, event | category | flops | bytes accessed | tf_op | source)
XLA Modules:
  0.0 125.8 jit_solution(5517854124214665056)
XLA Ops:
  0.6 120.6 %shard_map.169 = (bf16[150,2,512]{2,1,0:T(2,128)(2,1)}, bf16[150,2,512]{2,1,0:T(2,128)(2,1)}, f32[2,2,8]{2,1,0:T(2,128)}, f32[8,2304]{1,0:T(8,128)}, f32[512,512]{1,0:T(8,128)}, /*index=5*/f32[512,512]{1,0:T(8,128)}) custom-call(bf16[150,2,512]{2,1,0:T(2,128)(2,1)} %bitcast.10, bf16[150,2,512]{2,1,0:T(2,128)(2,1)} %bitcast.11, f32[1,2,512]{2,1,0:T(2,128)} %gains.1, ...), custom_call_target="tpu_custom_call" | custom-call | flops 10000000000 | bytes 10000000 | tf_op jit(solution)/shard_map/pallas_call | solution.py:923
  121.3 4.3 %shard_map.170 = (bf16[150,2,512]{2,1,0:T(2,128)(2,1)}, bf16[150,2,512]{2,1,0:T(2,128)(2,1)}, f32[1,2,8]{2,1,0:T(2,128)}, f32[1,2,8]{2,1,0:T(2,128)}, f32[1,8,15...) custom-call(bf16[150,2,512]{2,1,0:T(2,128)(2,1)} %get-tuple-element., ...), custom_call_target="tpu_custom_call" | custom-call | tf_op jit(solution)/shard_map/pallas_call | solution.py:946

commit v3 on v2

--- a/solution.py
+++ b/solution.py
@@ -83,11 +83,11 @@
     snd, rcv, rows_in, hidden, slope, acc, grows, gbuf, branch_kept, gblend, gpacked, small, extra_kept,
     part, part_in, part_acc, ring, ring_end,
     dense, dense_in, dense_acc, dense_dp, dense_out, dense_last,
-    second, second_in, second_far, second_out, second_last,
+    second, second_in, second_far, second_out, second_last, third, third_in, third_far,
     in_sem, w_send, w_recv, e_send, e_recv, r_send, f_send, t_send,
     a_send, a_recv, o_send, o_recv, o_loc,
     g_send, g_recv, h_send, h_recv, k_send, k_recv,
-    d_send, d_recv, dx_send, dx_recv, dy_send, dy_recv, sy_send, sy_recv, sx_send, sx_recv, fin_sem,
+    d_send, d_recv, dx_send, dx_recv, dy_send, dy_recv, sy_send, sy_recv, sx_send, sx_recv, ty_send, ty_recv, fin_sem,
 ):
     sections, experts, dps, tokens, features, cap, ffs, micro = dims
     images = tokens // SEQ
@@ -171,8 +171,9 @@
     load_x.wait()
     states[0] = nn(place[...], own_micro(xin)).astype(BF16)
     small[...] = jnp.zeros_like(small)
-    spare = first_width + second_width - 4 * features - EXTRA
-    second[:, pl.ds(second_width - spare, spare)] = jnp.zeros((features, spare), BF16)
+    query_width = first_width - EXTRA
+    rest_width = 3 * features - query_width
+    second[:, rest_width:] = jnp.zeros((features, second_width - rest_width), BF16)
 
     pl.semaphore_wait(barrier, 1 + 3 + len(OFFSETS))
 
@@ -316,12 +317,15 @@
     in_left = iota((total, span), 1) < HEAD_DIM
 
     def attention(l):
-        for i, (_, kept) in enumerate(dense_args):
-            arrived(kept.at[l], w_recv.at[l, i])
+        def need(*which):
+            for i in which:
+                arrived(dense_args[i][1].at[l], w_recv.at[l, i])
+        need(3, 4)
         current = states[l].astype(F32)
         norm, _ = normalized(current)
         normed = (norm * gn[l, 0:1] + bs[l, 0:1]).astype(BF16)
         norm1[l] = normed
+        need(0)
         packed[l] = nn(normed, wq[l]).astype(BF16)
         key_bias = jnp.where((iota((1, span), 1) & (ROWS - 1)) < SEQ, 0.0, -1e30)
         for p in range(pairs):
@@ -350,6 +354,7 @@
                 blended[l, i * ROWS:(i + 1) * ROWS, at:at + span] = nn(
                     low[i * ROWS:(i + 1) * ROWS], pair_keys(values, lane_side)
                 ).astype(BF16)
+        need(1)
         middle = current + nn(blended[l], wo[l])
         attended[l] = middle
         norm, _ = normalized(middle)
@@ -357,6 +362,7 @@
         norm2[l] = normed
         exchange_send(4 * l, 0, tn(s0[l] + s1[l], normed))
         spread = jnp.where(iota((EXTRA, experts), 0) == iota((EXTRA, experts), 1), 1.0, 0.0)
+        need(2)
         wr128[l] = nn(spread.astype(BF16), wr[l]).astype(BF16)
         logits = nt(normed, wr128[l])
         logits = jnp.where(iota((total, EXTRA), 1) < experts, logits, -1e30)
@@ -419,18 +425,19 @@
 
     def expert_weights(l):
         def block(step):
-            b = around(2 + step)
+            turn = 2 + step - 3 * (step // 2) - 2 * (step // 3)
+            b, c = around(turn), around(dps - turn)
             part[b, 0] = tn(rows_in[l], slope[l, b]).astype(BF16)
 
             @pl.when(s != l)
             def _():
                 part_copy(b, 0).start()
 
-            part[b, 1] = tn(hidden[l, b], grows[...]).astype(BF16)
+            part[c, 1] = tn(hidden[l, c], grows[...]).astype(BF16)
 
             @pl.when(s != l)
             def _():
-                part_copy(b, 1).start()
+                part_copy(c, 1).start()
         each(0, dps, block)
 
     def pair_part(b, k):
@@ -439,29 +446,33 @@
 
     def ring_copy(k):
         return remote(
-            part.at[far, k], ring.at[k], h_send.at[k], h_recv.at[k], (to_right, to_left)[k]
+            part_in.at[far, k], ring.at[k], h_send.at[k], h_recv.at[k], (to_right, to_left)[k]
         )
 
     def ring_last(way, k):
         return remote(
-            part.at[(right, left)[way], k], ring_end.at[way, k], k_send.at[way, k],
+            part_in.at[(right, left)[way], k], ring_end.at[way, k], k_send.at[way, k],
             k_recv.at[way, k], (to_right, to_left)[way],
         )
 
     def ring_first_step():
         for k in range(2):
-            part[far, k] = pair_part(far, k).astype(BF16)
+            part_in[far, k] = pair_part(far, k).astype(BF16)
             ring_copy(k).start()
+        for way, k in ((1, 0), (0, 1)):
+            b = (right, left)[way]
+            part_in[b, k] = pair_part(b, k).astype(BF16)
+            ring_last(way, k).start()
 
     def ring_second_step():
-        for way, k in ((0, 1), (1, 0), (0, 0), (1, 1)):
+        for way in range(2):
             b = (right, left)[way]
-            value = pair_part(b, k)
-            if way == k:
-                arrived(ring.at[k], h_recv.at[k])
-                value = value + ring[k].astype(F32)
-            part[b, k] = value.astype(BF16)
-            ring_last(way, k).start()
+            value = pair_part(b, way)
+            arrived(ring.at[way], h_recv.at[way])
+            part_in[b, way] = (value + ring[way].astype(F32)).astype(BF16)
+            ring_last(way, way).start()
+
+    def ring_own():
         for k in range(2):
             part_acc[k] = pair_part(d, k)
 
@@ -482,12 +493,15 @@
 
     def dense_dp_copy(j):
         return remote(
-            dense.at[around(j)], dense_dp.at[j - 1], dx_send.at[j - 1], dx_recv.at[j - 1],
+            dense_in.at[around(j)], dense_dp.at[j - 1], dx_send.at[j - 1], dx_recv.at[j - 1],
             (s, e, around(j)),
         )
 
     def second_twin():
         return remote(second, second_in, d_send.at[dps], d_recv.at[dps], twin)
+
+    def third_twin():
+        return remote(third, third_in, d_send.at[dps + 1], d_recv.at[dps + 1], twin)
 
     def second_dp_copy(j):
         return remote(
@@ -504,38 +518,40 @@
     def widen(values):
         return jnp.concatenate([values[:rows_own], values[rows_own:]], axis=1)
 
-    def dense_pair():
-        arrived(second_in, d_recv.at[dps])
+    def pair_rows(own, other, ends, send, recv):
         rows = rows_own * dps
 
         def pair(j):
             at = pl.ds(pl.multiple_of(j * rows, rows), rows)
-            second[at] = (second[at].astype(F32) + second_in[at].astype(F32)).astype(BF16)
+            other[at] = (own[at].astype(F32) + other[at].astype(F32)).astype(BF16)
         each(0, experts, pair)
         for y, z in OFFSETS:
             peer = expert_at(y, z)
             at = pl.ds(pl.multiple_of(peer * rows, rows), rows)
-            remote(second.at[at], second_far.at[e], sy_send, sy_recv, (s, peer, d)).start()
+            remote(other.at[at], ends.at[e], send, recv, (s, peer, d)).start()
         at = pl.ds(pl.multiple_of(e * rows, rows), rows)
-        pltpu.make_async_copy(second.at[at], second_far.at[e], sy_recv).start()
+        pltpu.make_async_copy(other.at[at], ends.at[e], recv).start()
+
+    def pair_third():
+        arrived(third_in, d_recv.at[dps + 1])
+        pair_rows(third, third_in, third_far, ty_send, ty_recv)
+
+    def pair_second():
+        arrived(second_in, d_recv.at[dps])
+        pair_rows(second, second_in, second_far, sy_send, sy_recv)
+
+    def pair_first():
         for j in (2, 1, 3):
             other = around(j)
             arrived(dense_in.at[other], d_recv.at[other])
-            dense[other] = (dense[other].astype(F32) + dense_in[other].astype(F32)).astype(BF16)
+            dense_in[other] = (
+                dense[other].astype(F32) + dense_in[other].astype(F32)
+            ).astype(BF16)
             dense_dp_copy(j).start()
         arrived(dense_in.at[d], d_recv.at[d])
         dense_acc[...] = dense[d].astype(F32) + dense_in[d].astype(F32)
 
     def dense_middle():
-        arrived(second_far, sy_recv)
-        arrived(second.at[pl.ds(0, features - rows_own * dps)], sy_send)
-        summed = second_far[0].astype(F32)
-        for j in range(1, experts):
-            summed = summed + second_far[j].astype(F32)
-        second_out[...] = narrow(summed.reshape(dps, rows_own, second_width))
-        for j in (2, 1, 3):
-            second_dp_copy(j).start()
-        pltpu.make_async_copy(second_out.at[d], second_last.at[d], sx_recv).start()
         for j in (1, 3, 2):
             copy = dense_dp_copy(j)
             copy.wait_send()
@@ -550,16 +566,24 @@
                 dense_out.at[peer], dense_last.at[e], dy_send, dy_recv, (s, peer, d)
             ).start()
         pltpu.make_async_copy(dense_out.at[e], dense_last.at[e], dy_recv).start()
+        arrived(third_far, ty_recv)
+        arrived(third_in.at[pl.ds(0, features - rows_own * dps)], ty_send)
+        late = third_far[0].astype(F32)
+        for j in range(1, experts):
+            late = late + third_far[j].astype(F32)
+        arrived(second_far, sy_recv)
+        arrived(second_in.at[pl.ds(0, features - rows_own * dps)], sy_send)
+        summed = second_far[0].astype(F32)
+        for j in range(1, experts):
+            summed = summed + second_far[j].astype(F32)
+        summed = jnp.concatenate([summed, late], axis=1)
+        second_out[...] = narrow(summed.reshape(dps, rows_own, summed.shape[1]))
+        for j in (2, 1, 3):
+            second_dp_copy(j).start()
+        pltpu.make_async_copy(second_out.at[d], second_last.at[d], sx_recv).start()
 
     def put(values, at):
         size = values.shape[1]
-        if at >= first_width:
-            second[:, pl.ds(at - first_width, size)] = values.astype(BF16)
-            return
-        if at + size > first_width:
-            put(values[:, first_width - at:], first_width)
-            values = values[:, :first_width - at]
-            size = first_width - at
         blocks = values.reshape(experts, dps, rows_own, size)
         for b in range(dps):
             dense[b, :, pl.ds(at, size)] = blocks[:, b].reshape(rows_dp, size).astype(BF16)
@@ -569,19 +593,25 @@
         lane = iota((8, EXTRA), 1)
         line = iota((8, EXTRA), 0)
         column = jnp.where((lane == line + experts) & (line < 4), 1.0, 0.0).astype(BF16)
-        put(extra_kept[l] + tn(high, column) + tn(low, column), 4 * features)
-
-    def put_dense(l):
-        put(tn(blended[l], branch_kept[...]), 3 * features)
-        put_extra(l)
-        for i in (2, 1):
-            put(tn(norm1[l], gpacked[:, i * features:(i + 1) * features]), i * features)
+        put(extra_kept[l] + tn(high, column) + tn(low, column), query_width)
+
+    def put_third(l):
+        third[...] = tn(blended[l], branch_kept[...]).astype(BF16)
+
+        @pl.when(s != l)
+        def _():
+            third_twin().start()
+
+    def put_second(l):
+        second[:, :rest_width] = tn(norm1[l], gpacked[:, query_width:]).astype(BF16)
 
         @pl.when(s != l)
         def _():
             second_twin().start()
 
-        put(tn(norm1[l], gpacked[:, :features]), 0)
+    def put_first(l):
+        put(tn(norm1[l], gpacked[:, :query_width]), 0)
+        put_extra(l)
 
         @pl.when(s != l)
         def _():
@@ -589,6 +619,7 @@
                 dense_twin(around(j)).start()
 
     def dense_twin_sent():
+        third_twin().wait_send()
         second_twin().wait_send()
         for b in range(dps):
             dense_twin(b).wait_send()
@@ -604,7 +635,7 @@
         extra_kept[l] = tn(norm2[l], high) + tn(norm2[l], low)
         return nn(high, wr128[l]) + nn(low, wr128[l])
 
-    def attention_back(l, way, grad_y, from_gate, between):
+    def attention_back(l, way, grad_y, from_gate, before, between):
         back = exchange_recv(4 * l + 3, way)
         grad_normed = nn(s0[l] + s1[l], back) + from_gate
         norm, root = normalized(attended[l])
@@ -613,6 +644,7 @@
         grad_att = grad_y + norm_back(grad_normed, norm, root, gn[l, 1:2])
         branch = grad_att.astype(BF16)
         branch_kept[...] = branch
+        before()
         gblend[...] = nt(branch, wo[l]).astype(BF16)
         for p in range(pairs):
             at = p * span
@@ -706,17 +738,20 @@
     def _():
         ring_first_step()
 
-    kept = attention_back(1, 1, grad_y, from_gate, lambda: None)
+    kept = attention_back(1, 1, grad_y, from_gate, lambda: None, lambda: None)
     finish_back(1, *kept)
 
     gates = gate_parts(0)
     grad_y = gbuf[...].astype(F32)
     slot_grads(0, 0, grad_y, gates[4], gates[5])
-    put_dense(1)
+    put_third(1)
+    put_second(1)
+    put_first(1)
 
     @pl.when(s == 1)
     def _():
         ring_second_step()
+        ring_own()
 
     hand_out(0, 1, stage_out, states[2])
     hand_out(1, 1, stage_grad, gbuf[...])
@@ -727,32 +762,35 @@
     def _():
         part_sent()
 
+    expert_weights(0)
+
+    @pl.when(s == 0)
+    def _():
+        ring_first_step()
+        dense_twin_sent()
+
     @pl.when(s == 1)
     def _():
-        ring_sent()
-
-    expert_weights(0)
-
-    @pl.when(s == 0)
-    def _():
-        ring_first_step()
-
-    @pl.when(s == 1)
-    def _():
-        dense_pair()
+        pair_third()
+        pair_second()
+        pair_first()
 
     def between():
+        put_second(0)
+
         @pl.when(s == 0)
         def _():
             ring_second_step()
-            dense_twin_sent()
-
-        @pl.when(s == 1)
-        def _():
-            dense_middle()
-
-    kept = attention_back(0, 0, grad_y, from_gate, between)
-    put_dense(0)
+            pair_third()
+            pair_second()
+
+    kept = attention_back(0, 0, grad_y, from_gate, lambda: put_third(0), between)
+    put_first(0)
+
+    @pl.when(s == 0)
+    def _():
+        pair_first()
+
     finish_back(0, *kept)
     hand_out(1, 0, stage_grad, gbuf[...])
     keep_out = join(0, stage_out, join_out, o_outs)
@@ -760,8 +798,9 @@
 
     @pl.when(s == 0)
     def _():
-        dense_pair()
-        dense_middle()
+        ring_own()
+
+    dense_middle()
 
     for k in range(2):
         for way in range(2):
@@ -781,7 +820,7 @@
         widen(jnp.sum(second_last[...].astype(F32), axis=0)),
     ], axis=1)
     o_dense[...] = final
-    tail = final[:, 4 * features: 4 * features + EXTRA]
+    tail = final[:, query_width:first_width]
     tail_high, tail_low = split_sum(tail)
     tail_low, tail_rest = split_sum(tail - tail_high.astype(F32))
 
@@ -806,9 +845,7 @@
         for j in range(1, dps):
             expert_forward(i, j).wait_send()
 
-    @pl.when(s == 0)
-    def _():
-        ring_sent()
+    ring_sent()
 
     @pl.when(s == 1)
     def _():
@@ -847,9 +884,13 @@
         load.start()
     o_gain[0] = norms[0]
     o_bias[0] = norms[1]
-    o_qkv[0] = dense[:, : 3 * features]
-    o_attn[0] = dense[:, 3 * features: 4 * features]
-    o_router[0] = dense[:, 4 * features: 4 * features + o_router.shape[-1]]
+    width = dense.shape[-1]
+    first = width * 2 // 9
+    query = first - EXTRA
+    o_qkv[0, :, :query] = dense[:, :query]
+    o_qkv[0, :, query:] = dense[:, first: first + 3 * features - query]
+    o_attn[0] = dense[:, width - features:]
+    o_router[0] = dense[:, query: query + o_router.shape[-1]]
     for load, copy in zip(loads, copies):
         load.wait()
         copy.start()
@@ -867,7 +908,7 @@
     rows_dp = features // dps
     rows_own = rows_dp // experts
     width = -(-(4 * features + EXTRA) // 256) * 256
-    first = width // 3
+    first = width * 2 // 9
     second = width - first
     half = features // 2
     block = ffs // dps
@@ -910,15 +951,17 @@
         V((dps, rows_dp, first), BF16), V((dps, rows_dp, first), BF16),
         V((rows_dp, first), F32), V((dps - 1, rows_dp, first), BF16),
         V((experts, 2 * rows_own, first // 2), BF16), V((experts, 2 * rows_own, first // 2), BF16),
-        V((features, second), BF16), V((features, second), BF16),
-        V((experts, dps * rows_own, second), BF16),
+        V((features, second - features), BF16), V((features, second - features), BF16),
+        V((experts, dps * rows_own, second - features), BF16),
         V((dps, 2 * rows_own, second // 2), BF16), V((dps, 2 * rows_own, second // 2), BF16),
+        V((features, features), BF16), V((features, features), BF16),
+        V((experts, dps * rows_own, features), BF16),
         dma((2,)), dma((6,)), dma((2, 6)), dma((2, 2)), dma((2, 2, dps)), dma((2,)),
         dma((2, dps - 1)), dma((2,)),
         dma((2,)), dma((8,)), dma((2,)), dma((2,)), dma((2,)),
         dma((dps, 2)), dma((dps, 2)), dma((2,)), dma((2,)), dma((2, 2)), dma((2, 2)),
-        dma((dps + 1,)), dma((dps + 1,)), dma((dps - 1,)), dma((dps - 1,)), dma, dma, dma, dma,
-        dma((dps - 1,)), dma, dma((2,)),
+        dma((dps + 2,)), dma((dps + 2,)), dma((dps - 1,)), dma((dps - 1,)), dma, dma, dma, dma,
+        dma((dps - 1,)), dma, dma, dma, dma((2,)),
     ]
     made = pl.pallas_call(
         partial(kernel, dims),

time: 126 us -> 118 us (0.937)
  Pallas kernels: 125 us -> 117 us
    pallas_call x1, Pallas kernels: 121 us -> 113 us  [local(): pl.pallas_call(partial(kernel, dims), out_shape=(out(tokens, micro, featu...]
where the time goes in v3:
time: 118 us
  Pallas kernels  117 us (99%)
    pallas_call x1, Pallas kernels, local(): pl.pallas_call(partial(kernel, dims), out_shape=(out(tokens, micro, featu...  113 us
    pallas_call x1, Pallas kernels, local(): pl.pallas_call(partial(finish, features), out_shape=(out(tokens, micro, f...  4.33 us

profile of v3, /device:TPU:0, one launch (start us, length us, event | category | flops | bytes accessed | tf_op | source)
XLA Modules:
  0.0 117.7 jit_solution(4005977777867141094)
XLA Ops:
  0.6 112.5 %shard_map.169 = (bf16[150,2,512]{2,1,0:T(2,128)(2,1)}, bf16[150,2,512]{2,1,0:T(2,128)(2,1)}, f32[2,2,8]{2,1,0:T(2,128)}, f32[8,2304]{1,0:T(8,128)}, f32[512,512]{1,0:T(8,128)}, /*index=5*/f32[512,512]{1,0:T(8,128)}) custom-call(bf16[150,2,512]{2,1,0:T(2,128)(2,1)} %bitcast.10, bf16[150,2,512]{2,1,0:T(2,128)(2,1)} %bitcast.11, f32[1,2,512]{2,1,0:T(2,128)} %gains.1, ...), custom_call_target="tpu_custom_call" | custom-call | flops 10000000000 | bytes 10000000 | tf_op jit(solution)/shard_map/pallas_call | solution.py:966
  113.2 4.3 %shard_map.170 = (bf16[150,2,512]{2,1,0:T(2,128)(2,1)}, bf16[150,2,512]{2,1,0:T(2,128)(2,1)}, f32[1,2,8]{2,1,0:T(2,128)}, f32[1,2,8]{2,1,0:T(2,128)}, f32[1,8,15...) custom-call(bf16[150,2,512]{2,1,0:T(2,128)(2,1)} %get-tuple-element., ...), custom_call_target="tpu_custom_call" | custom-call | tf_op jit(solution)/shard_map/pallas_call | solution.py:989

commit v4 on v3

--- a/solution.py
+++ b/solution.py
@@ -374,33 +374,42 @@
 
     def expert_forward_pass(l):
         rows_in[l] = exchange_recv(4 * l, 0)
-        acc[...] = jnp.zeros_like(acc)
-
-        def block(step):
-            b = block_at(step)
-
-            @pl.when((s == l) & (step == 0))
+        order = (d, right, left, far)
+
+        def need(step):
+            b = order[step]
+
+            @pl.when(s == l)
             def _():
-                for i, (_, kept) in enumerate(expert_args):
-                    arrived(kept.at[l, d], e_recv.at[i, l, d])
-
-            @pl.when((s == l) & (step == 3))
-            def _():
-                for i, (_, kept) in enumerate(expert_args):
-                    arrived(kept.at[l, far], e_recv.at[i, l, far])
-                    expert_forward(i, 2).start()
+                if step == 0:
+                    for i, (_, kept) in enumerate(expert_args):
+                        arrived(kept.at[l, d], e_recv.at[i, l, d])
+                if step == 3:
+                    for i, (_, kept) in enumerate(expert_args):
+                        arrived(kept.at[l, far], e_recv.at[i, l, far])
+                        expert_forward(i, 2).start()
 
             @pl.when(s != l)
             def _():
                 for i, (_, kept) in enumerate(expert_args):
                     arrived(kept.at[l, b], e_recv.at[i, l, b])
 
-            after, dslope = gelu_parts(nn(rows_in[l], wi[l, b]))
+        need(0)
+        need(1)
+        pre = nn(rows_in[l], wi[l, d])
+        for step in range(dps):
+            if step + 1 < dps:
+                if step:
+                    need(step + 1)
+                later = nn(rows_in[l], wi[l, order[step + 1]])
+            b = order[step]
+            after, dslope = gelu_parts(pre)
             after = after.astype(BF16)
             hidden[l, b] = after
             slope[l, b] = dslope.astype(BF16)
-            acc[...] += nn(after, wu[l, b])
-        each(0, dps, block)
+            term = nn(after, wu[l, b])
+            acc[...] = term if step == 0 else acc[...] + term
+            pre = later
         exchange_send(4 * l + 1, 0, acc[...])
 
     def slot_grads(l, way, grad_y, gate0, gate1):
@@ -417,7 +426,8 @@
             before = (nt(grows[...], wu[l, b]) * slope[l, b].astype(F32)).astype(BF16)
             slope[l, b] = before
             acc[...] += nt(before, wi[l, b])
-        each(0, dps, block)
+        for b in range(dps):
+            block(b)
         exchange_send(4 * l + 3, way, acc[...])
 
     def part_copy(b, k):

time: 118 us -> 117 us (level)
  no operation moved by 1% of the time
where the time goes in v4:
time: 117 us
  Pallas kernels  116 us (99%)
    pallas_call x1, Pallas kernels, local(): pl.pallas_call(partial(kernel, dims), out_shape=(out(tokens, micro, featu...  112 us
    pallas_call x1, Pallas kernels, local(): pl.pallas_call(partial(finish, features), out_shape=(out(tokens, micro, f...  4.33 us

profile of v4, /device:TPU:0, one launch (start us, length us, event | category | flops | bytes accessed | tf_op | source)
XLA Modules:
  0.0 117.1 jit_solution(7011426464373852650)
XLA Ops:
  0.6 112.0 %shard_map.169 = (bf16[150,2,512]{2,1,0:T(2,128)(2,1)}, bf16[150,2,512]{2,1,0:T(2,128)(2,1)}, f32[2,2,8]{2,1,0:T(2,128)}, f32[8,2304]{1,0:T(8,128)}, f32[512,512]{1,0:T(8,128)}, /*index=5*/f32[512,512]{1,0:T(8,128)}) custom-call(bf16[150,2,512]{2,1,0:T(2,128)(2,1)} %bitcast.10, bf16[150,2,512]{2,1,0:T(2,128)(2,1)} %bitcast.11, f32[1,2,512]{2,1,0:T(2,128)} %gains.1, ...), custom_call_target="tpu_custom_call" | custom-call | flops 10000000000 | bytes 10000000 | tf_op jit(solution)/shard_map/pallas_call | solution.py:976
  112.6 4.3 %shard_map.170 = (bf16[150,2,512]{2,1,0:T(2,128)(2,1)}, bf16[150,2,512]{2,1,0:T(2,128)(2,1)}, f32[1,2,8]{2,1,0:T(2,128)}, f32[1,2,8]{2,1,0:T(2,128)}, f32[1,8,15...) custom-call(bf16[150,2,512]{2,1,0:T(2,128)(2,1)} %get-tuple-element., ...), custom_call_target="tpu_custom_call" | custom-call | tf_op jit(solution)/shard_map/pallas_call | solution.py:999
